TPU v7x, 32 devices: a whole 2x2x4 slice. The times are simulated.
32 devices in a mesh: section: 2 (over core), ctx: 4 (over z), tp: 4 (over y, x).
Axes of the slice: x: 2, y: 2, z: 4, core: 2. Of those that a mesh axis runs over, the one named last changes fastest.
Arguments:
- inputs: bfloat16 [2, 2048, 2048], P(None, 'ctx'), may hold values from -6 to 6
- cotangent: bfloat16 [2, 2048, 2048], P(None, 'ctx'), may hold values from -6 to 6
- lengths: int32 [2, 3], replicated, may hold values from 1 to 1792, 2048 in all within a row
- norm_gains: float32 [2, 2, 2048], P('section'), may hold values from 0.5 to 1.5
- norm_shifts: float32 [2, 2, 2048], P('section'), may hold values from -1.5 to 1.5
- qkv_weight: bfloat16 [2, 3, 2048, 2048], P('section', None, 'ctx', 'tp'), may hold values from -0.125 to 0.125
- qkv_bias: float32 [2, 3, 2048], P('section', None, 'tp'), may hold values from -1.5 to 1.5
- out_weight: bfloat16 [2, 2048, 2048], P('section', 'tp', 'ctx'), may hold values from -2 to 2
- gate_up_weight: bfloat16 [2, 2, 2048, 5632], P('section', None, 'ctx', 'tp'), may hold values from -0.125 to 0.125
- down_weight: bfloat16 [2, 5632, 2048], P('section', 'tp', 'ctx'), may hold values from -0.078125 to 0.078125
Outputs:
- layer_outputs: bfloat16 [2, 2, 2048, 2048], P('section', None, 'ctx')
- input_grads: float32 [2, 2, 2048, 2048], P('section', None, 'ctx')
- norm_gain_grads: float32 [2, 2, 2048], P('section')
- norm_shift_grads: float32 [2, 2, 2048], P('section')
- qkv_weight_grads: float32 [2, 3, 2048, 2048], P('section', None, 'ctx', 'tp')
- qkv_bias_grads: float32 [2, 3, 2048], P('section', None, 'tp')
- out_weight_grads: float32 [2, 2048, 2048], P('section', 'tp', 'ctx')
- gate_up_grads: float32 [2, 2, 2048, 5632], P('section', None, 'ctx', 'tp')
- down_grads: float32 [2, 5632, 2048], P('section', 'tp', 'ctx')
Inputs may be any that keep to these rules, and one draw needn't show every extreme that they name: In each micro-batch the 3 lengths sum to 2048, and one of them, at a place drawn from the seed, is 1792.
All inputs are finite; a program needn't handle non-finite values.
Results may differ from a plain program's by a relative error of at most 0.025.
Values may be sent and summed in bfloat16 or wider, within the bound.
No kernel may reach another device: no remote copies, remote signals or barrier semaphores. Data moves between devices by JAX's collectives and lax.ppermute only.
A program may use at most 320 MiB of HBM per device.

v0:
```python
import math

import jax
import jax.numpy as jnp
from jax import lax
from jax.experimental import pallas as pl
from jax.experimental.pallas import tpu as pltpu
from jax.sharding import PartitionSpec as P

HEAD_DIM = 64
ROTATED_ENTRIES = 16
EPSILON = 1e-05
NEGATIVE = -1e30
ROTARY_BASE = 10000.0
LANES = 128
F32 = jnp.float32
BF16 = jnp.bfloat16
CONTRACT_LAST = (((1,), (1,)), ((), ()))
CONTRACT_FIRST = (((0,), (0,)), ((), ()))
VMEM_BYTES = 48 * 1024 * 1024


def head_rows(values, head):
    lane = lax.broadcasted_iota(jnp.int32, values.shape, 1)
    return jnp.where(lane // HEAD_DIM == head, values, 0.0).astype(BF16)


def attend_kernel(chunks, flags, query_ref, bias_ref, *refs):
    full_ref, low_ref, log_ref, high, total, summed = refs[chunks:]
    rows = query_ref.shape[0]
    heads = LANES // HEAD_DIM
    scaled = query_ref[...].astype(F32) * HEAD_DIM**-0.5
    queries = [head_rows(scaled, head) for head in range(heads)]
    high[...] = jnp.full(high.shape, NEGATIVE, F32)
    total[...] = jnp.zeros(total.shape, F32)
    summed[...] = jnp.zeros(summed.shape, F32)
    for chunk in range(chunks):

        @pl.when(flags[chunk] != 0)
        def _():
            keys = refs[chunk][0]
            values = refs[chunk][1]
            for head in range(heads):
                scores = lax.dot_general(
                    keys, queries[head], CONTRACT_LAST, preferred_element_type=F32
                )
                scores = scores + bias_ref[chunk * rows : (chunk + 1) * rows, :]
                old = high[head]
                new = jnp.maximum(old, jnp.max(scores, axis=0, keepdims=True))
                weights = jnp.exp(scores - new)
                decay = jnp.exp(old - new)
                total[head] = total[head] * decay + jnp.sum(weights, axis=0, keepdims=True)
                summed[head] = summed[head] * decay + lax.dot_general(
                    values, weights.astype(BF16), CONTRACT_FIRST, preferred_element_type=F32
                )
                high[head] = new

    row = lax.broadcasted_iota(jnp.int32, (LANES, rows), 0)
    merged = jnp.zeros((LANES, rows), F32)
    for head in range(heads):
        merged = jnp.where(row // HEAD_DIM == head, summed[head] / total[head], merged)
        log_ref[0, head : head + 1, :] = high[head] + jnp.log(total[head])
    merged = merged.T
    full_ref[...] = merged
    low_ref[...] = merged.astype(BF16)


def column_spec(rows):
    return pl.BlockSpec((rows, LANES), lambda pair, flags: (0, pair))


def double_spec(rows):
    return pl.BlockSpec((2, rows, LANES), lambda pair, flags: (0, 0, pair))


def attend(queries, key_values, bias, flags):
    rows, width = queries.shape
    chunks = len(key_values)
    pairs = width // LANES
    heads = LANES // HEAD_DIM
    own = column_spec(rows)
    return pl.pallas_call(
        lambda *refs: attend_kernel(chunks, *refs),
        out_shape=(
            jax.ShapeDtypeStruct((rows, width), F32),
            jax.ShapeDtypeStruct((rows, width), BF16),
            jax.ShapeDtypeStruct((pairs, heads, rows), F32),
        ),
        grid_spec=pltpu.PrefetchScalarGridSpec(
            num_scalar_prefetch=1,
            grid=(pairs,),
            in_specs=[own, pl.BlockSpec(bias.shape, lambda pair, flags: (0, 0))]
            + [double_spec(rows)] * chunks,
            out_specs=(
                own,
                own,
                pl.BlockSpec((1, heads, rows), lambda pair, flags: (pair, 0, 0)),
            ),
            scratch_shapes=[
                pltpu.VMEM((heads, 1, rows), F32),
                pltpu.VMEM((heads, 1, rows), F32),
                pltpu.VMEM((heads, LANES, rows), F32),
            ],
        ),
        compiler_params=pltpu.CompilerParams(vmem_limit_bytes=VMEM_BYTES),
        cost_estimate=pl.CostEstimate(
            flops=4 * chunks * rows * rows * width * 2,
            bytes_accessed=2 * chunks * rows * width * 2 + bias.size * 4,
            transcendentals=0,
        ),
        name="attend",
    )(flags, queries, bias, *key_values)


def attend_back_kernel(chunks, flags, query_ref, bias_ref, grad_ref, full_ref, log_ref, *refs):
    query_grad_ref = refs[chunks]
    grad_refs = refs[chunks + 1 : 2 * chunks + 1]
    summed = refs[2 * chunks + 1]
    rows = query_ref.shape[0]
    heads = LANES // HEAD_DIM
    scale = HEAD_DIM**-0.5
    scaled = query_ref[...].astype(F32) * scale
    grad = grad_ref[...].astype(F32)
    product = (grad * full_ref[...]).T
    queries = [head_rows(scaled, head) for head in range(heads)]
    grads = [head_rows(grad, head) for head in range(heads)]
    deltas = [
        jnp.sum(product[head * HEAD_DIM : (head + 1) * HEAD_DIM, :], axis=0, keepdims=True)
        for head in range(heads)
    ]
    summed[...] = jnp.zeros(summed.shape, F32)
    for chunk in range(chunks):

        @pl.when(flags[chunk] != 0)
        def _():
            keys = refs[chunk][0]
            values = refs[chunk][1]
            key_float = keys.astype(F32)
            key_grad = jnp.zeros((rows, LANES), F32)
            value_grad = jnp.zeros((rows, LANES), F32)
            query_grad = summed[...]
            for head in range(heads):
                scores = lax.dot_general(
                    keys, queries[head], CONTRACT_LAST, preferred_element_type=F32
                )
                scores = scores + bias_ref[chunk * rows : (chunk + 1) * rows, :]
                weights = jnp.exp(scores - log_ref[0, head : head + 1, :])
                weight_grad = lax.dot_general(
                    values, grads[head], CONTRACT_LAST, preferred_element_type=F32
                )
                score_grad = (weights * (weight_grad - deltas[head])).astype(BF16)
                value_grad = value_grad + jnp.dot(
                    weights.astype(BF16), grads[head], preferred_element_type=F32
                )
                key_grad = key_grad + jnp.dot(
                    score_grad, queries[head], preferred_element_type=F32
                )
                query_grad = query_grad + lax.dot_general(
                    head_rows(key_float, head),
                    score_grad,
                    CONTRACT_FIRST,
                    preferred_element_type=F32,
                )
            summed[...] = query_grad
            grad_refs[chunk][0] = key_grad.astype(BF16)
            grad_refs[chunk][1] = value_grad.astype(BF16)

        @pl.when(flags[chunk] == 0)
        def _():
            grad_refs[chunk][...] = jnp.zeros((2, rows, LANES), BF16)

    query_grad_ref[...] = summed[...].T * scale


def attend_back(queries, key_values, bias, flags, grad, full, log_total):
    rows, width = queries.shape
    chunks = len(key_values)
    pairs = width // LANES
    heads = LANES // HEAD_DIM
    own = column_spec(rows)
    results = pl.pallas_call(
        lambda *refs: attend_back_kernel(chunks, *refs),
        out_shape=[jax.ShapeDtypeStruct((rows, width), F32)]
        + [jax.ShapeDtypeStruct((2, rows, width), BF16)] * chunks,
        grid_spec=pltpu.PrefetchScalarGridSpec(
            num_scalar_prefetch=1,
            grid=(pairs,),
            in_specs=[
                own,
                pl.BlockSpec(bias.shape, lambda pair, flags: (0, 0)),
                own,
                own,
                pl.BlockSpec((1, heads, rows), lambda pair, flags: (pair, 0, 0)),
            ]
            + [double_spec(rows)] * chunks,
            out_specs=[own] + [double_spec(rows)] * chunks,
            scratch_shapes=[pltpu.VMEM((LANES, rows), F32)],
        ),
        compiler_params=pltpu.CompilerParams(vmem_limit_bytes=VMEM_BYTES),
        cost_estimate=pl.CostEstimate(
            flops=10 * chunks * rows * rows * width * 2,
            bytes_accessed=4 * chunks * rows * width * 2 + bias.size * 4,
            transcendentals=0,
        ),
        name="attend_back",
    )(flags, queries, bias, grad, full, log_total, *key_values)
    return results[0], results[1:]


def swap_cores(block):
    return lax.ppermute(block, "section", [(0, 1), (1, 0)])


def exchange(block, axis, bit):
    return lax.ppermute(block, axis, [(i, i ^ bit) for i in range(lax.axis_size(axis))])


def after(value, *others):
    return lax.optimization_barrier((value, others))[0]


def tp_scatter(partial):
    ranks = lax.axis_size("tp")
    rows, width = partial.shape
    pieces = partial.reshape(ranks, rows // ranks, width)
    total = pieces[0].astype(F32)
    for k in range(1, ranks):
        total = total + exchange(pieces[k], "tp", k).astype(F32)
    return total


def tp_gather(piece):
    ranks = lax.axis_size("tp")
    return jnp.concatenate([piece] + [exchange(piece, "tp", k) for k in range(1, ranks)], axis=0)


def across(blocks, bit, upward):
    count = lax.axis_size("ctx")
    pairs = [(i, i ^ bit) for i in range(count)]
    if bit == count // 4:
        pairs = [(i, j) for i, j in pairs if (step_of(i, count) < step_of(j, count)) == upward]
    return [lax.ppermute(block, "ctx", pairs) for block in blocks]


def step_of(index, count):
    return index if index < count // 2 else count - 1 - index


def gather_chunks(own):
    count = lax.axis_size("ctx")
    blocks = [own]
    bit = 1
    while bit < count // 2:
        blocks = blocks + across(blocks, bit, True)
        bit *= 2
    arrived = [swap_cores(block) for block in blocks]
    return [block for pair in zip(blocks, arrived) for block in pair]


def scatter_chunks(blocks):
    count = lax.axis_size("ctx")
    arrived = [swap_cores(block) for block in blocks[1::2]]
    blocks = [
        mine.astype(F32) + other.astype(F32) for mine, other in zip(blocks[::2], arrived)
    ]
    bit = count // 4
    while bit >= 1:
        arrived = across([block.astype(BF16) for block in blocks[bit:]], bit, False)
        blocks = [mine + other.astype(F32) for mine, other in zip(blocks[:bit], arrived)]
        bit //= 2
    return blocks[0]


def norm_forward(values, gain, shift):
    mean = jnp.mean(values, axis=1, keepdims=True)
    centred = values - mean
    spread = jnp.mean(centred * centred, axis=1, keepdims=True)
    inverse = lax.rsqrt(spread + EPSILON)
    return (centred * inverse * gain + shift).astype(BF16), (mean, inverse)


def norm_backward(values, statistics, gain, grad):
    mean, inverse = statistics
    hat = (values - mean) * inverse
    scaled = gain * grad
    first = jnp.mean(scaled, axis=1, keepdims=True)
    second = jnp.mean(scaled * hat, axis=1, keepdims=True)
    moved = inverse * (scaled - first - hat * second)
    return moved, jnp.sum(grad * hat, axis=0), jnp.sum(grad, axis=0)


def rotary_tables(local_place, width):
    half = ROTATED_ENTRIES // 2
    entry = jnp.arange(HEAD_DIM)
    frequency = jnp.exp(
        -((entry % half).astype(F32) * 2.0 / ROTATED_ENTRIES) * math.log(ROTARY_BASE)
    )
    frequency = jnp.where(entry < ROTATED_ENTRIES, frequency, 0.0)
    angle = local_place.astype(F32)[:, None] * frequency[None, :]
    sine = jnp.sin(angle)
    tables = (
        jnp.cos(angle),
        jnp.where(entry < half, -sine, 0.0),
        jnp.where(entry >= half, sine, 0.0),
    )
    return tuple(jnp.tile(table, (1, width // HEAD_DIM)) for table in tables)


def rotate(values, tables, sign):
    half = ROTATED_ENTRIES // 2
    cosine, low, high = tables
    return (
        values * cosine
        + jnp.roll(values, -half, axis=1) * (low * sign)
        + jnp.roll(values, half, axis=1) * (high * sign)
    )


def dot(left, right):
    return jnp.dot(left, right, preferred_element_type=F32)


def dot_back(left, right):
    return lax.dot_general(left, right, CONTRACT_LAST, preferred_element_type=F32)


def token_sum(left, right):
    return lax.dot_general(left, right, CONTRACT_FIRST, preferred_element_type=F32)


def into(values, halves):
    middle = values.shape[1] // 2
    return dot(values[:, :middle], halves[0]) + dot(values[:, middle:], halves[1])


def out_of(values, halves):
    return jnp.concatenate([dot_back(values, half).astype(BF16) for half in halves], axis=1)


def all_sum(value, axes):
    for axis in axes:
        bit = 1
        while bit < lax.axis_size(axis):
            value = value + exchange(value, axis, bit)
            bit *= 2
    return value


def project_forward(normed, weights, bias_row, layout):
    tables, mask, flags = layout

    def project(c):
        return into(normed, [half[c] for half in weights]) + bias_row[c][None]

    key_value = jnp.stack([rotate(project(1), tables, 1.0).astype(BF16), project(2).astype(BF16)])
    key_values = gather_chunks(key_value)
    return rotate(project(0), tables, 1.0).astype(BF16), key_values


def attention_forward(piece, queries, key_values, out_weights, layout):
    tables, mask, flags = layout
    attended, attended_low, log_total = attend(queries, key_values, mask, flags)
    partial = out_of(attended_low, [half[0] for half in out_weights])
    hidden = piece.astype(F32) + tp_scatter(partial)
    return hidden, (queries, key_values, attended, attended_low, log_total)


def gate_forward(normed, weights):
    gate, up = [into(normed, [half[c] for half in weights]) for c in range(2)]
    activated = (gate * jax.nn.sigmoid(gate) * up).astype(BF16)
    return gate, up, activated


def down_forward(hidden, activated, weights):
    partial = out_of(activated, [half[0] for half in weights])
    return (hidden + tp_scatter(partial)).astype(BF16)


def shared_weight_grad(own, other):
    arrived = swap_cores(other.astype(BF16))
    return (own + arrived.astype(F32)).astype(BF16)


def weight_grad(values, grads):
    middle = values.shape[1] // 2
    own, other = [
        jnp.stack([token_sum(half, grad) for grad in grads])
        for half in (values[:, :middle], values[:, middle:])
    ]
    return shared_weight_grad(own, other)


def scatter_weight_grad(total):
    return lax.psum_scatter(total, "ctx", scatter_dimension=1, tiled=True)


def gate_backward(grad_full, kept, down):
    gate, up, activated = kept
    activated_grad = into(grad_full, [half[0] for half in down])
    sigmoid = jax.nn.sigmoid(gate)
    swish = gate * sigmoid
    gate_grad = (activated_grad * up * (sigmoid * (1.0 + gate * (1.0 - sigmoid)))).astype(BF16)
    up_grad = (activated_grad * swish).astype(BF16)
    return gate_grad, up_grad


def feed_partial(gate_grad, up_grad, weights):
    return jnp.concatenate(
        [
            (dot_back(gate_grad, half[0]) + dot_back(up_grad, half[1])).astype(BF16)
            for half in weights
        ],
        axis=1,
    )


def projected_partial(projected, weights):
    return jnp.concatenate(
        [
            sum(dot_back(part, half[c]) for c, part in enumerate(projected)).astype(BF16)
            for half in weights
        ],
        axis=1,
    )


def body(
    inputs,
    cotangent,
    lengths,
    norm_gains,
    norm_shifts,
    qkv_weight,
    qkv_bias,
    out_weight,
    gate_up_weight,
    down_weight,
):
    core = lax.axis_index("section")
    place_index = lax.axis_index("ctx")
    rank = lax.axis_index("tp")
    ranks = lax.axis_size("tp")
    count = lax.axis_size("ctx")
    rows, features = inputs.shape[1:]
    width = qkv_weight.shape[3]
    far = count // 2
    batch = place_index // far
    position = 2 * jnp.where(batch == 0, place_index, count - 1 - place_index) + core
    first_core = core == 0
    both = ("section", "ctx")
    piece_rows = rows // ranks

    def by_core(zero, one):
        return jnp.where(first_core, zero, one)

    def pick(array, index, axis=0):
        return lax.dynamic_index_in_dim(array, index, axis, keepdims=False)

    def reorder(block):
        pieces = block.reshape(ranks, piece_rows, -1)
        return jnp.concatenate(
            [pick(pieces, jnp.bitwise_xor(rank, k)) for k in range(ranks)], axis=0
        )

    def split(array):
        cut = array.reshape(array.shape[:-1] + (count, 2, features // (2 * count)))
        shape = array.shape[:-1] + (features // 2,)
        axis = cut.ndim - 2
        return jnp.concatenate(
            [pick(cut, index, axis).reshape(shape) for index in (core, 1 - core)], axis=-1
        )

    def unsplit(array):
        lead = array.shape[:-1]
        cut = array.reshape(lead + (2, count, features // (2 * count)))
        first, second = [lax.index_in_dim(cut, j, len(lead), keepdims=False) for j in range(2)]
        joined = jnp.stack([by_core(first, second), by_core(second, first)], axis=len(lead) + 1)
        return joined.reshape(lead + (features,))

    def seat(index, half):
        step = index // 2
        return (index % 2) * count + (step if half == 0 else count - 1 - step)

    def take_in(array):
        piece = pick(pick(array, core).reshape(ranks, piece_rows, features), rank)
        pairs = [(half * count + i, seat(i, half)) for half in range(2) for i in range(count)]
        return split(lax.ppermute(piece, both, pairs))

    def send_home(layer, piece):
        piece = unsplit(piece)
        return jnp.stack(
            [
                lax.ppermute(piece, both, [(seat(i, half), layer * count + i) for i in range(count)])
                for half in range(2)
            ]
        )

    def spread_home(layer, own):
        blocks = [own]
        for k in range(1, ranks):
            pairs = [(layer * ranks + i, layer * ranks + (i ^ k)) for i in range(ranks)]
            blocks.append(lax.ppermute(own, ("section", "tp"), pairs))
        return blocks

    def assemble(blocks, dtype):
        whole = jnp.zeros((2, rows, features), dtype)
        for k, block in enumerate(blocks):
            start_row = jnp.bitwise_xor(rank, k) * piece_rows
            whole = lax.dynamic_update_slice_in_dim(
                whole, block.astype(dtype), start_row, axis=1
            )
        return whole[None]

    length_row = pick(lengths, batch)
    ends = jnp.cumsum(length_row)
    inner = jnp.arange(rows, dtype=jnp.int32)
    inner = jnp.bitwise_xor(inner // piece_rows, rank) * piece_rows + inner % piece_rows

    def documents(place):
        passed = ends[None, :] <= place[:, None]
        document = jnp.sum(passed.astype(jnp.int32), axis=1)
        begins = jnp.sum(jnp.where(passed, length_row[None, :], 0), axis=1)
        return document, place - begins

    query_place = position * rows + inner
    query_document, local_place = documents(query_place)
    tables = rotary_tables(local_place, width)
    masks = []
    for index in range(count):
        key_place = jnp.bitwise_xor(position, index) * rows + inner
        key_document, ignored = documents(key_place)
        masks.append(
            (key_document[:, None] == query_document[None, :])
            & (key_place[:, None] <= query_place[None, :])
        )
    flags = jnp.stack([jnp.any(mask) for mask in masks]).astype(jnp.int32)
    mask = jnp.where(jnp.concatenate(masks, axis=0), 0.0, NEGATIVE).astype(F32)
    layout = (tables, mask, flags)

    def both_layers(array):
        arrived = swap_cores(array)
        return [by_core(array, arrived), by_core(arrived, array)]

    gains = [split(array) for array in both_layers(norm_gains[0])]
    shifts = [split(array) for array in both_layers(norm_shifts[0])]
    biases = both_layers(qkv_bias[0])

    def shard_halves(shard):
        half = shard.shape[1] // 2
        kept = lax.dynamic_slice_in_dim(shard, core * half, half, 1)
        arrived = swap_cores(lax.dynamic_slice_in_dim(shard, (1 - core) * half, half, 1))
        return [by_core(kept, arrived), by_core(arrived, kept)]

    def gather(piece, *others):
        return lax.all_gather(after(piece, *others), "ctx", axis=1, tiled=True)

    def halves(own, *others):
        own = after(own, *others)
        return own, swap_cores(own)

    qkv_shards = shard_halves(qkv_weight[0])
    out_shards = shard_halves(out_weight[0].T[None])
    gate_up_shards = shard_halves(gate_up_weight[0])
    down_shards = shard_halves(down_weight[0].T[None])

    start = take_in(inputs)
    normed_zero, statistics_zero = norm_forward(start.astype(F32), gains[0][0], shifts[0][0])
    normed_zero = tp_gather(normed_zero)
    attention_zero = gather(jnp.concatenate([qkv_shards[0], out_shards[0]], axis=0))
    attention_zero, normed_zero, layout = lax.optimization_barrier(
        (attention_zero, normed_zero, layout)
    )
    feed_zero = gather(jnp.concatenate([gate_up_shards[0], down_shards[0]], axis=0))
    attention_one = gather(
        jnp.concatenate([qkv_shards[1], out_shards[1]], axis=0), attention_zero
    )
    attention_halves = halves(attention_zero)
    qkv_weights = [[half[:3] for half in attention_halves], None]
    out_weights = [[half[3:] for half in attention_halves], None]
    queries_zero, key_values_zero = project_forward(normed_zero, qkv_weights[0], biases[0], layout)
    hidden_zero, kept_attention_zero = attention_forward(
        start, queries_zero, key_values_zero, out_weights[0], layout
    )
    second_zero, second_statistics_zero = norm_forward(hidden_zero, gains[0][1], shifts[0][1])
    second_zero = tp_gather(second_zero)
    grad = take_in(after(cotangent, normed_zero))
    grad_full = tp_gather(after(grad, second_zero))
    feed_zero, second_zero, grad_full = lax.optimization_barrier((feed_zero, second_zero, grad_full))
    gate_up_one = gather(gate_up_shards[1], feed_zero)
    feed_halves = halves(feed_zero)
    gate_up_weights = [[half[:2] for half in feed_halves], None]
    down_weights = [[half[2:] for half in feed_halves], None]
    kept_feed_zero = gate_forward(second_zero, gate_up_weights[0])
    middle = down_forward(hidden_zero, kept_feed_zero[2], down_weights[0])
    normed_one, statistics_one = norm_forward(middle.astype(F32), gains[1][0], shifts[1][0])
    normed_one = tp_gather(normed_one)
    attention_one, normed_one = lax.optimization_barrier((attention_one, normed_one))
    down_one = gather(down_shards[1], attention_one)
    attention_halves = halves(attention_one)
    qkv_weights[1] = [half[:3] for half in attention_halves]
    out_weights[1] = [half[3:] for half in attention_halves]
    queries_one, key_values_one = project_forward(normed_one, qkv_weights[1], biases[1], layout)
    hidden_one, kept_attention_one = attention_forward(
        middle, queries_one, key_values_one, out_weights[1], layout
    )
    second_one, second_statistics_one = norm_forward(hidden_one, gains[1][1], shifts[1][1])
    second_one = tp_gather(second_one)
    gate_up_one, second_one = lax.optimization_barrier((gate_up_one, second_one))
    gate_up_weights[1] = halves(gate_up_one)
    kept_feed_one = gate_forward(second_one, gate_up_weights[1])
    home_zero = send_home(0, after(middle, second_one))

    kept_feed = (kept_feed_zero, kept_feed_one)
    kept_attention = (kept_attention_zero, kept_attention_one)
    second_norm = (
        (hidden_zero, second_statistics_zero, gains[0][1]),
        (hidden_one, second_statistics_one, gains[1][1]),
    )
    first_norm = (
        (start.astype(F32), statistics_zero, gains[0][0]),
        (middle.astype(F32), statistics_one, gains[1][0]),
    )
    first_normed = (normed_zero, normed_one)
    second_normed = (second_zero, second_one)
    input_grads = [None, None]
    small_grads = [None, None]
    scattered = [None, None]
    tables, mask, flags = layout
    for layer in (1, 0):
        down_total = weight_grad(grad_full, [kept_feed[layer][2]])
        if layer == 1:
            down_one, down_total, grad_full = lax.optimization_barrier(
                (down_one, down_total, grad_full)
            )
            down_weights[1] = halves(down_one)
        gate_grad, up_grad = gate_backward(grad_full, kept_feed[layer], down_weights[layer])
        partial = feed_partial(gate_grad, up_grad, gate_up_weights[layer])
        down_grad = scatter_weight_grad(down_total)
        second_grad = tp_scatter(partial)
        gate_total = weight_grad(second_normed[layer], [gate_grad])
        second_grad, gate_total = lax.optimization_barrier((second_grad, gate_total))
        moved, gain_second, shift_second = norm_backward(*second_norm[layer], second_grad)
        hidden_grad = grad.astype(F32) + moved
        branch_grad = tp_gather(hidden_grad.astype(BF16))
        up_total = weight_grad(second_normed[layer], [up_grad])
        branch_grad, up_total = lax.optimization_barrier((branch_grad, up_total))
        if layer == 1:
            branch_grad, home_zero = lax.optimization_barrier((branch_grad, home_zero))
            home_zero = spread_home(0, home_zero)
        if layer == 0:
            branch_grad = after(branch_grad, attention_grad)
        queries, key_values, attended, attended_low, log_total = kept_attention[layer]
        attended_grad = into(branch_grad, [half[0] for half in out_weights[layer]]).astype(BF16)
        if layer == 0:
            last = down_forward(
                hidden_one, after(kept_feed_one[2], attended_grad), down_weights[1]
            )
        query_grad, key_value_grads = attend_back(
            queries, key_values, mask, flags, attended_grad, attended, log_total
        )
        query_grad, key_value_grads = after((query_grad, key_value_grads), down_grad)
        gate_weight_grad = scatter_weight_grad(gate_total)
        key_value_grad = after(scatter_chunks(key_value_grads), gate_weight_grad)
        up_weight_grad = scatter_weight_grad(after(up_total, key_value_grad))
        if layer == 0:
            home_one = send_home(1, after(jnp.concatenate([last, input_grads[1]]), query_grad))
            key_value_grad, home_one = lax.optimization_barrier((key_value_grad, home_one))
            home_one = spread_home(1, home_one)
        out_total = weight_grad(branch_grad, [attended_low])
        query_grad = rotate(query_grad, tables, -1.0).astype(BF16)
        key_value_grad, out_total, query_grad = lax.optimization_barrier(
            (key_value_grad, out_total, query_grad)
        )
        if layer == 1:
            key_value_grad, home_zero = lax.optimization_barrier((key_value_grad, home_zero))
        key_grad = rotate(key_value_grad[0], tables, -1.0).astype(BF16)
        projected = (query_grad, key_grad, key_value_grad[1].astype(BF16))
        partial = projected_partial(projected, qkv_weights[layer])
        first_grad = tp_scatter(partial)
        qkv_total = weight_grad(first_normed[layer], projected)
        first_grad, qkv_total = lax.optimization_barrier((first_grad, qkv_total))
        bias_grad = jnp.stack([jnp.sum(part.astype(F32), axis=0) for part in projected])
        moved, gain_first, shift_first = norm_backward(*first_norm[layer], first_grad)
        grad = (hidden_grad + moved).astype(BF16)
        input_grads[layer] = grad
        attention_total = jnp.concatenate([qkv_total, out_total])
        if layer == 0:
            home_grad, home_one, attention_total = lax.optimization_barrier(
                (send_home(0, grad), home_one, attention_total)
            )
        attention_grad = scatter_weight_grad(attention_total)
        if layer == 1:
            grad_full = after(tp_gather(grad), up_weight_grad)
        norm_grads = unsplit(jnp.stack([gain_first, gain_second, shift_first, shift_second]))
        small_grads[layer] = (norm_grads, bias_grad)
        gate_up_grad = jnp.concatenate([gate_weight_grad, up_weight_grad])
        scattered[layer] = (attention_grad, gate_up_grad, down_grad)

    norm_grads, bias_grads = [
        jnp.stack(parts) for parts in zip(*[after(small, attention_total) for small in small_grads])
    ]
    norm_rows = norm_grads.size // LANES
    packed = jnp.concatenate(
        [all_sum(norm_grads.reshape(-1, LANES), ("tp",)), bias_grads.reshape(-1, LANES)]
    )
    packed = all_sum(packed, ("section",))
    packed = packed + sum(exchange(packed, "ctx", k) for k in range(1, count))
    norm_grads = packed[:norm_rows].reshape(norm_grads.shape)
    bias_grads = packed[norm_rows:].reshape(bias_grads.shape)
    norm_grads, bias_grads = by_core(norm_grads[0], norm_grads[1]), by_core(bias_grads[0], bias_grads[1])
    home_grad = spread_home(0, home_grad)
    layer_outputs = assemble(
        [by_core(zero, one[:, :piece_rows]) for zero, one in zip(home_zero, home_one)], BF16
    )
    grad_outputs = assemble(
        [by_core(zero, one[:, piece_rows:]) for zero, one in zip(home_grad, home_one)], F32
    )

    def join_halves(zero, one):
        to_zero = lax.ppermute(zero, "section", [(1, 0)])
        to_one = lax.ppermute(one, "section", [(0, 1)])
        low = by_core(zero, to_one)
        high = by_core(to_zero, one)
        return jnp.concatenate([low, high], axis=1).astype(F32)

    joined = [join_halves(zero, one) for zero, one in zip(*scattered)]
    return (
        layer_outputs,
        grad_outputs,
        norm_grads[None, :2],
        norm_grads[None, 2:],
        joined[0][None, :3],
        bias_grads[None],
        joined[0][3].T[None],
        joined[1][None],
        joined[2][0].T[None],
    )


def solution(mesh):
    placed = (
        P(None, "ctx", None),
        P(None, "ctx", None),
        P(),
        P("section", None, None),
        P("section", None, None),
        P("section", None, "ctx", "tp"),
        P("section", None, "tp"),
        P("section", "tp", "ctx"),
        P("section", None, "ctx", "tp"),
        P("section", "tp", "ctx"),
    )
    return jax.shard_map(
        body,
        mesh=mesh,
        in_specs=placed,
        out_specs=(
            P("section", None, "ctx", None),
            P("section", None, "ctx", None),
            P("section", None, None),
            P("section", None, None),
            P("section", None, "ctx", "tp"),
            P("section", None, "tp"),
            P("section", "tp", "ctx"),
            P("section", None, "ctx", "tp"),
            P("section", "tp", "ctx"),
        ),
        check_vma=False,
    )
```

profile of v0, /device:TPU:0, one launch (start us, length us, event | category | flops | bytes accessed | tf_op | source)
XLA Modules:
  0.0 1253.2 jit_solution(16416347153288757981)
XLA Ops:
  59.7 12.0 collective-permute-done.6
  73.3 32.1 %all-gather.6.cloned.1.call-done = bf16[4,1024,512]{2,1,0:T(8,128)(2,1)} async-done(((bf16[4,256,512]{2,1,0:T(8,128)(2,1)}), bf16[4,1024,512]{2,1,0:T(8,128)(2,1)}) %all-gather.6.cloned.1.call-update) | async-done | bytes 4194320 | tf_op jit(solution)/shard_map/all_gather | solution.py:555
  133.6 45.3 %collective-permute-done.11.refs_5_.refs_8_ = bf16[2,512,512]{2,1,0:T(8,128)(2,1)S(1)} collective-permute-done((bf16[2,512,512]{2,1,0:T(8,128)(2,1)S(1)}, bf16[2,512,512]{2,1,0:T(8,128)(2,1)S(1)}, u32[]{:S(2)}, u32[]{:S(2)}) %collective-permute-start.11) | collective-permute-done | bytes 1048608 | tf_op jit(solution)/shard_map/ppermute | solution.py:242
  208.4 9.7 collective-permute-done.15
  271.9 16.6 %all-gather.10.cloned.1.call-done = bf16[3,1024,1408]{2,1,0:T(8,128)(2,1)} async-done(((bf16[3,256,1408]{2,1,0:T(8,128)(2,1)}), bf16[3,1024,1408]{2,1,0:T(8,128)(2,1)}) %all-gather.10.cloned.1.call-update) | async-done | bytes 8650768 | tf_op jit(solution)/shard_map/all_gather | solution.py:555
  324.2 11.3 collective-permute-done.26
  335.5 11.8 collective-permute-done.27
  352.5 11.4 collective-permute-done.29
  363.9 10.5 collective-permute-done.30
  399.5 45.5 %collective-permute-done.34.refs_5_.refs_8_ = bf16[2,512,512]{2,1,0:T(8,128)(2,1)S(1)} collective-permute-done((bf16[2,512,512]{2,1,0:T(8,128)(2,1)S(1)}, bf16[2,512,512]{2,1,0:T(8,128)(2,1)S(1)}, u32[]{:S(2)}, u32[]{:S(2)}) %collective-permute-start.34) | collective-permute-done | bytes 1048608 | tf_op jit(solution)/shard_map/ppermute | solution.py:242
  474.6 9.6 collective-permute-done.38
  544.3 41.5 %all-gather.12.cloned.1.call-done = bf16[1,1024,1408]{2,1,0:T(8,128)(2,1)} async-done(((bf16[1,256,1408]{2,1,0:T(8,128)(2,1)}), bf16[1,1024,1408]{2,1,0:T(8,128)(2,1)}) %all-gather.12.cloned.1.call-update) | async-done | bytes 2883600 | tf_op jit(solution)/shard_map/all_gather | solution.py:555
  639.0 11.2 collective-permute-done.46
  671.3 10.3 collective-permute-done.50
  686.5 12.8 %attend_back.2 = (f32[512,512]{1,0:T(8,128)S(1)}, bf16[2,512,512]{2,1,0:T(8,128)(2,1)S(1)}, bf16[2,512,512]{2,1,0:T(8,128)(2,1)S(1)}, bf16[2,512,512]{2,1,0:T(8,128)(2,1)S(1)}, bf16[2,512,512]{2,1,0:T(8,128)(2,1)}) custom-call(s32[4]{0:T(128)S(1)} %add_convert_fusion.14.refs_0_, bf16[512,512]{1,0:T(8,128)(2,1)S(1)} %copy-done.5, ...), custom_call_target="tpu_custom_call" | custom-call | flops 10737418240 | bytes 12582912 | tf_op jit(solution)/shard_map/attend_back/pallas_call | solution.py:181
  721.0 32.3 %collective-permute-done.57 = bf16[2,512,512]{2,1,0:T(8,128)(2,1)S(1)} collective-permute-done((bf16[2,512,512]{2,1,0:T(8,128)(2,1)S(1)}, bf16[2,512,512]{2,1,0:T(8,128)(2,1)S(1)}, u32[]{:S(2)}, u32[]{:S(2)}) %collective-permute-start.57) | collective-permute-done | bytes 1048608 | tf_op jit(solution)/shard_map/ppermute | solution.py:242
  788.3 10.5 collective-permute-done.63
  810.9 11.4 collective-permute-done.66
  883.4 10.3 collective-permute-done.69
  929.6 10.5 collective-permute-done.74
  958.0 12.8 %attend_back.3 = (f32[512,512]{1,0:T(8,128)S(1)}, bf16[2,512,512]{2,1,0:T(8,128)(2,1)S(1)}, bf16[2,512,512]{2,1,0:T(8,128)(2,1)S(1)}, bf16[2,512,512]{2,1,0:T(8,128)(2,1)S(1)}, bf16[2,512,512]{2,1,0:T(8,128)(2,1)}) custom-call(s32[4]{0:T(128)S(1)} %add_convert_fusion.14.refs_0_, bf16[512,512]{1,0:T(8,128)(2,1)S(1)} %copy-done.3, ...), custom_call_target="tpu_custom_call" | custom-call | flops 10737418240 | bytes 12582912 | tf_op jit(solution)/shard_map/attend_back/pallas_call | solution.py:181
  1016.7 31.3 %collective-permute-done.80 = bf16[2,512,512]{2,1,0:T(8,128)(2,1)S(1)} collective-permute-done((bf16[2,512,512]{2,1,0:T(8,128)(2,1)S(1)}, bf16[2,512,512]{2,1,0:T(8,128)(2,1)S(1)}, u32[]{:S(2)}, u32[]{:S(2)}) %collective-permute-start.80) | collective-permute-done | bytes 1048608 | tf_op jit(solution)/shard_map/ppermute | solution.py:242
  1128.5 15.9 %collective-permute-done.92 = bf16[128,2048]{1,0:T(8,128)(2,1)} collective-permute-done((bf16[128,2048]{1,0:T(8,128)(2,1)}, bf16[128,2048]{1,0:T(8,128)(2,1)}, u32[]{:S(2)}, u32[]{:S(2)}) %collective-permute-start.92) | collective-permute-done | bytes 524320 | tf_op jit(solution)/shard_map/ppermute | solution.py:493
  1209.2 13.4 %collective-permute-done.97 = bf16[2,128,2048]{2,1,0:T(8,128)(2,1)} collective-permute-done((bf16[2,128,2048]{2,1,0:T(8,128)(2,1)S(1)}, bf16[2,128,2048]{2,1,0:T(8,128)(2,1)}, u32[]{:S(2)}, u32[]{:S(2)}) %collective-permute-start.97) | collective-permute-done | bytes 1048608 | tf_op jit(solution)/shard_map/ppermute | solution.py:502
  (879 shorter events, 796.3 us)
Async XLA Ops:
  7.2 98.2 %all-gather.6.cloned.1.call-start = ((), (), s32[]{:S(2)}) async-start(), calls=%async_computation.8 | async-start | bytes 5242880 | tf_op jit(solution)/shard_map/all_gather | solution.py:555
  26.1 262.4 %all-gather.10.cloned.1.call-start = ((), (), s32[]{:S(2)}) async-start(), calls=%async_computation.10 | async-start | bytes 10813440 | tf_op jit(solution)/shard_map/all_gather | solution.py:555
  32.7 74.0 %collective-permute-start.16 = (bf16[2,256,1408]{2,1,0:T(8,128)(2,1)}, bf16[2,256,1408]{2,1,0:T(8,128)(2,1)}, u32[]{:S(2)}, u32[]{:S(2)}) collective-permute-start(bf16[2,256,1408]{2,1,0:T(8,128)(2,1)} %dynamic-slice_bitcast_fusion), channel_id=1, source_target_pairs={{0,16},{16,0},{1,17},{17,1},{2,18},{18,2},{3,19},{19,3},{4,20},{20... | collective-permute-start | bytes 4325384 | tf_op jit(solution)/shard_map/ppermute | solution.py:211
  112.1 269.7 %all-gather.8.cloned.1.call-start = ((), (), s32[]{:S(2)}) async-start(), calls=%async_computation.9 | async-start | bytes 5242880 | tf_op jit(solution)/shard_map/all_gather | solution.py:555
  131.8 47.1 %collective-permute-start.11 = (bf16[2,512,512]{2,1,0:T(8,128)(2,1)S(1)}, bf16[2,512,512]{2,1,0:T(8,128)(2,1)S(1)}, u32[]{:S(2)}, u32[]{:S(2)}) collective-permute-start(bf16[2,512,512]{2,1,0:T(8,128)(2,1)S(1)} %pad_maximum_fusion.16.refs_3_.refs_6_), channel_id=1, source_target_pairs={{0,4},{12,8},{1,5},{13,9},{2,6},{14,10},{3,7},{15,11},{16,20},{28,... | collective-permute-start | bytes 3145736 | tf_op jit(solution)/shard_map/ppermute | solution.py:242
  292.9 215.7 %all-gather.14.cloned.1.call-start = ((), (), s32[]{:S(2)}) async-start(), calls=%async_computation.12 | async-start | bytes 7208960 | tf_op jit(solution)/shard_map/all_gather | solution.py:555
  381.9 203.9 %all-gather.12.cloned.1.call-start = ((), (), s32[]{:S(2)}) async-start(), calls=%async_computation.11 | async-start | bytes 3604480 | tf_op jit(solution)/shard_map/all_gather | solution.py:555
  398.0 47.1 %collective-permute-start.34 = (bf16[2,512,512]{2,1,0:T(8,128)(2,1)S(1)}, bf16[2,512,512]{2,1,0:T(8,128)(2,1)S(1)}, u32[]{:S(2)}, u32[]{:S(2)}) collective-permute-start(bf16[2,512,512]{2,1,0:T(8,128)(2,1)S(1)} %pad_maximum_fusion.17.refs_3_.refs_6_), channel_id=1, source_target_pairs={{0,4},{12,8},{1,5},{13,9},{2,6},{14,10},{3,7},{15,11},{16,20},{28,... | collective-permute-start | bytes 3145736 | tf_op jit(solution)/shard_map/ppermute | solution.py:242
  514.0 186.3 %reduce-scatter.9.cloned.1.call-start = ((), (), s32[]{:S(2)}) async-start(), calls=%async_computation.13 | async-start | bytes 3604480 | tf_op jit(solution)/shard_map/reduce_scatter | solution.py:394
  597.6 157.5 %reduce-scatter.11.cloned.1.call-start = ((), (), s32[]{:S(2)}) async-start(), calls=%async_computation.14 | async-start | bytes 3604480 | tf_op jit(solution)/shard_map/reduce_scatter | solution.py:394
  653.9 180.3 %reduce-scatter.13.cloned.1.call-start = ((), (), s32[]{:S(2)}) async-start(), calls=%async_computation.15 | async-start | bytes 3604480 | tf_op jit(solution)/shard_map/reduce_scatter | solution.py:394
  705.5 49.7 %collective-permute-start.59 = (bf16[2,128,2048]{2,1,0:T(8,128)(2,1)}, bf16[2,128,2048]{2,1,0:T(8,128)(2,1)}, u32[]{:S(2)}, u32[]{:S(2)}) collective-permute-start(bf16[2,128,2048]{2,1,0:T(8,128)(2,1)} %pad_maximum_fusion.18), channel_id=1, source_target_pairs={{0,1},{1,0},{2,3},{3,2},{4,5},{5,4},{6,7},{7,6},{8,9},{9,8},{10,11... | collective-permute-start | bytes 3145736 | tf_op jit(solution)/shard_map/ppermute | solution.py:502
  755.1 186.6 %reduce-scatter.15.cloned.1.call-start = ((), (), s32[]{:S(2)}) async-start(), calls=%async_computation.16 | async-start | bytes 5242880 | tf_op jit(solution)/shard_map/reduce_scatter | solution.py:394
  803.8 177.0 %reduce-scatter.17.cloned.1.call-start = ((), (), s32[]{:S(2)}) async-start(), calls=%async_computation.17 | async-start | bytes 3604480 | tf_op jit(solution)/shard_map/reduce_scatter | solution.py:394
  854.9 194.8 %reduce-scatter.19.cloned.1.call-start = ((), (), s32[]{:S(2)}) async-start(), calls=%async_computation.18 | async-start | bytes 3604480 | tf_op jit(solution)/shard_map/reduce_scatter | solution.py:394
  860.7 57.8 %collective-permute-start.76 = (bf16[1,1024,1408]{2,1,0:T(8,128)(2,1)}, bf16[1,1024,1408]{2,1,0:T(8,128)(2,1)}, u32[]{:S(2)}, u32[]{:S(2)}) collective-permute-start(bf16[1,1024,1408]{2,1,0:T(8,128)(2,1)} %fusion.12), channel_id=1, source_target_pairs={{0,16},{16,0},{1,17},{17,1},{2,18},{18,2},{3,19},{19,3},{4,20},{20... | collective-permute-start | bytes 8650760 | tf_op jit(solution)/shard_map/ppermute | solution.py:211
  893.7 225.2 %collective-permute-start.109 = (bf16[1,256,1408]{2,1,0:T(8,128)(2,1)}, bf16[1,256,1408]{2,1,0:T(8,128)(2,1)}, u32[]{:S(2)}, u32[]{:S(2)}) collective-permute-start(bf16[1,256,1408]{2,1,0:T(8,128)(2,1)} %reduce-scatter.9.cloned.1.call-done), channel_id=1, source_target_pairs={{0,16},{1,17},{2,18},{3,19},{4,20},{5,21},{6,22},{7,23},{8,24},{9,... | collective-permute-start | bytes 2162696 | tf_op jit(solution)/shard_map/ppermute | solution.py:721
  918.3 288.3 %reduce-scatter.23.cloned.1.call-start = ((), (), s32[]{:S(2)}) async-start(), calls=%async_computation.20 | async-start | bytes 3604480 | tf_op jit(solution)/shard_map/reduce_scatter | solution.py:394
  1060.0 172.6 %reduce-scatter.21.cloned.1.call-start = ((), (), s32[]{:S(2)}) async-start(), calls=%async_computation.19 | async-start | bytes 5242880 | tf_op jit(solution)/shard_map/reduce_scatter | solution.py:394
  1088.6 60.5 %collective-permute-start.93 = (bf16[2,256,2048]{2,1,0:T(8,128)(2,1)}, bf16[2,256,2048]{2,1,0:T(8,128)(2,1)}, u32[]{:S(2)}, u32[]{:S(2)}) collective-permute-start(bf16[2,256,2048]{2,1,0:T(8,128)(2,1)} %pad_maximum_fusion.13), channel_id=1, source_target_pairs={{16,17},{17,16},{18,19},{19,18},{20,21},{21,20},{22,23},{23,22},{2... | collective-permute-start | bytes 6291464 | tf_op jit(solution)/shard_map/ppermute | solution.py:502
  1099.0 50.1 %collective-permute-start.94 = (bf16[2,256,2048]{2,1,0:T(8,128)(2,1)}, bf16[2,256,2048]{2,1,0:T(8,128)(2,1)}, u32[]{:S(2)}, u32[]{:S(2)}) collective-permute-start(bf16[2,256,2048]{2,1,0:T(8,128)(2,1)} %pad_maximum_fusion.13), channel_id=1, source_target_pairs={{16,18},{17,19},{18,16},{19,17},{20,22},{21,23},{22,20},{23,21},{2... | collective-permute-start | bytes 6291464 | tf_op jit(solution)/shard_map/ppermute | solution.py:502
  1101.1 48.1 %collective-permute-start.95 = (bf16[2,256,2048]{2,1,0:T(8,128)(2,1)}, bf16[2,256,2048]{2,1,0:T(8,128)(2,1)S(1)}, u32[]{:S(2)}, u32[]{:S(2)}) collective-permute-start(bf16[2,256,2048]{2,1,0:T(8,128)(2,1)} %pad_maximum_fusion.13), channel_id=1, source_target_pairs={{16,19},{17,18},{18,17},{19,16},{20,23},{21,22},{22,21},{23,20},{2... | collective-permute-start | bytes 6291464 | tf_op jit(solution)/shard_map/ppermute | solution.py:502
  1144.4 84.3 %collective-permute-start.107 = (bf16[2,256,1408]{2,1,0:T(8,128)(2,1)}, bf16[2,256,1408]{2,1,0:T(8,128)(2,1)}, u32[]{:S(2)}, u32[]{:S(2)}) collective-permute-start(bf16[2,256,1408]{2,1,0:T(8,128)(2,1)} %constant_dynamic-update-slice_fusion.14), channel_id=1, source_target_pairs={{0,16},{1,17},{2,18},{3,19},{4,20},{5,21},{6,22},{7,23},{8,24},{9,... | collective-permute-start | bytes 4325384 | tf_op jit(solution)/shard_map/ppermute | solution.py:721
  1154.7 48.5 %collective-permute-start.96 = (bf16[2,128,2048]{2,1,0:T(8,128)(2,1)}, bf16[2,128,2048]{2,1,0:T(8,128)(2,1)}, u32[]{:S(2)}, u32[]{:S(2)}) collective-permute-start(bf16[2,128,2048]{2,1,0:T(8,128)(2,1)} %pad_maximum_fusion.21), channel_id=1, source_target_pairs={{0,1},{1,0},{2,3},{3,2},{4,5},{5,4},{6,7},{7,6},{8,9},{9,8},{10,11... | collective-permute-start | bytes 3145736 | tf_op jit(solution)/shard_map/ppermute | solution.py:502
  (246 other events, 4645.0 us)
Sparse Core Ops, SparseCore 0:
  26.2 79.1 all-gather.5
  112.3 176.1 all-gather.9
  293.0 88.8 all-gather.7
  383.9 123.8 all-gather.13
  514.2 71.6 all-gather.11
  597.7 56.7 reduce-scatter.8
  657.3 59.8 reduce-scatter.10
  755.2 53.2 reduce-scatter.12
  811.4 76.6 reduce-scatter.14
  890.9 56.6 reduce-scatter.16
  950.6 56.0 reduce-scatter.18
  1060.1 58.3 reduce-scatter.22
  1149.3 83.2 reduce-scatter.20
where the time goes:
time: 1270 us; the launch traced here: 1250 us
  waiting for transfers between devices  598 us (47%)
  matrix products  216 us (17%)
  starting transfers between devices  155 us (12%)
  other arithmetic  127 us (10%)
  local copies, waits for them, and re-layouts  95.7 us (8%)
  Pallas kernels  44.1 us (3%)
  between operations  17.2 us (1%)
    ppermute x54, waiting for transfers between devices, exchange(): lax.ppermute(block, axis, [(i, i ^ bit) for i in range(lax.axis_size(axis...  297 us
    ppermute x4, waiting for transfers between devices, across(): return [lax.ppermute(block, 'ctx', pairs) for block in blocks]  154 us
    all_gather x5, waiting for transfers between devices, gather(): return lax.all_gather(after(piece, *others), 'ctx', axis=1, tiled=True)  96.1 us
    dot_general x28, matrix products, dot(): return jnp.dot(left, right, preferred_element_type=F32)  86.3 us
    dot_general x28, matrix products, token_sum(): lax.dot_general(left, right, CONTRACT_FIRST, preferred_element_type=F32)  69.6 us
    ppermute x54, starting transfers between devices, exchange(): lax.ppermute(block, axis, [(i, i ^ bit) for i in range(lax.axis_size(axis...  63.2 us
    dot_general x28, matrix products, dot_back(): lax.dot_general(left, right, CONTRACT_LAST, preferred_element_type=F32)  60.2 us
    unnamed x312, local copies, waits for them, and re-layouts  30.1 us
  transfers between devices with their start and end apart: 124, of which 57 were waited for; matrix products, arithmetic and copies ran while one was open for 32% of the time, Pallas kernels for 4%

commit v1 on v0

--- a/solution.py
+++ b/solution.py
@@ -219,19 +219,45 @@
     return lax.optimization_barrier((value, others))[0]
 
 
-def tp_scatter(partial):
+def tp_scatter(halves):
     ranks = lax.axis_size("tp")
-    rows, width = partial.shape
-    pieces = partial.reshape(ranks, rows // ranks, width)
-    total = pieces[0].astype(F32)
-    for k in range(1, ranks):
-        total = total + exchange(pieces[k], "tp", k).astype(F32)
-    return total
+    rows, width = halves[0].shape
+    first, second = [half.reshape(ranks, rows // ranks, width) for half in halves]
+    if ranks != 4:
+        both = jnp.concatenate([first, second], axis=2)
+        total = both[0].astype(F32)
+        for k in range(1, ranks):
+            total = total + exchange(both[k], "tp", k).astype(F32)
+        return total
+    near = exchange(jnp.stack([first[1], first[3]]), "tp", 1).astype(F32)
+    far = exchange(second[2:], "tp", 2).astype(F32)
+    across_first = exchange((first[2].astype(F32) + near[1]).astype(BF16), "tp", 2)
+    across_second = exchange((second[1].astype(F32) + far[1]).astype(BF16), "tp", 1)
+    return jnp.concatenate(
+        [
+            first[0].astype(F32) + near[0] + across_first.astype(F32),
+            second[0].astype(F32) + far[0] + across_second.astype(F32),
+        ],
+        axis=1,
+    )
 
 
 def tp_gather(piece):
     ranks = lax.axis_size("tp")
-    return jnp.concatenate([piece] + [exchange(piece, "tp", k) for k in range(1, ranks)], axis=0)
+    middle = piece.shape[1] // 2
+    first, second = piece[:, :middle], piece[:, middle:]
+    if ranks != 4:
+        blocks = [piece] + [exchange(piece, "tp", k) for k in range(1, ranks)]
+        whole = jnp.concatenate(blocks, axis=0)
+        return [whole[:, :middle], whole[:, middle:]]
+    first_far = exchange(first, "tp", 2)
+    second_near = exchange(second, "tp", 1)
+    first_rest = exchange(jnp.stack([first, first_far]), "tp", 1)
+    second_rest = exchange(jnp.concatenate([second, second_near]), "tp", 2)
+    return [
+        jnp.concatenate([first, first_rest[0], first_far, first_rest[1]]),
+        jnp.concatenate([second, second_near, second_rest]),
+    ]
 
 
 def across(blocks, bit, upward):
@@ -329,12 +355,11 @@
 
 
 def into(values, halves):
-    middle = values.shape[1] // 2
-    return dot(values[:, :middle], halves[0]) + dot(values[:, middle:], halves[1])
+    return dot(values[0], halves[0]) + dot(values[1], halves[1])
 
 
 def out_of(values, halves):
-    return jnp.concatenate([dot_back(values, half).astype(BF16) for half in halves], axis=1)
+    return [dot_back(values, half).astype(BF16) for half in halves]
 
 
 def all_sum(value, axes):
@@ -346,19 +371,34 @@
     return value
 
 
-def project_forward(normed, weights, bias_row, layout):
-    tables, mask, flags = layout
-
-    def project(c):
-        return into(normed, [half[c] for half in weights]) + bias_row[c][None]
-
-    key_value = jnp.stack([rotate(project(1), tables, 1.0).astype(BF16), project(2).astype(BF16)])
-    key_values = gather_chunks(key_value)
-    return rotate(project(0), tables, 1.0).astype(BF16), key_values
+def earlier_chip(normed_piece):
+    if lax.axis_size("ctx") != 4:
+        return None
+    return across([normed_piece], 1, True)[0]
+
+
+def project_forward(normed, earlier, weights, bias_row, layout):
+    tables, earlier_tables, mask, flags = layout
+
+    def project(rows, c):
+        return into(rows, [half[c] for half in weights]) + bias_row[c][None]
+
+    def key_value(rows, turn):
+        return jnp.stack(
+            [rotate(project(rows, 1), turn, 1.0).astype(BF16), project(rows, 2).astype(BF16)]
+        )
+
+    own = key_value(normed, tables)
+    if earlier is None:
+        key_values = gather_chunks(own)
+    else:
+        blocks = [own, key_value(earlier, earlier_tables)]
+        key_values = [each for block in blocks for each in (block, swap_cores(block))]
+    return rotate(project(normed, 0), tables, 1.0).astype(BF16), key_values
 
 
 def attention_forward(piece, queries, key_values, out_weights, layout):
-    tables, mask, flags = layout
+    tables, earlier_tables, mask, flags = layout
     attended, attended_low, log_total = attend(queries, key_values, mask, flags)
     partial = out_of(attended_low, [half[0] for half in out_weights])
     hidden = piece.astype(F32) + tp_scatter(partial)
@@ -382,11 +422,7 @@
 
 
 def weight_grad(values, grads):
-    middle = values.shape[1] // 2
-    own, other = [
-        jnp.stack([token_sum(half, grad) for grad in grads])
-        for half in (values[:, :middle], values[:, middle:])
-    ]
+    own, other = [jnp.stack([token_sum(half, grad) for grad in grads]) for half in values]
     return shared_weight_grad(own, other)
 
 
@@ -405,23 +441,17 @@
 
 
 def feed_partial(gate_grad, up_grad, weights):
-    return jnp.concatenate(
-        [
-            (dot_back(gate_grad, half[0]) + dot_back(up_grad, half[1])).astype(BF16)
-            for half in weights
-        ],
-        axis=1,
-    )
+    return [
+        (dot_back(gate_grad, half[0]) + dot_back(up_grad, half[1])).astype(BF16)
+        for half in weights
+    ]
 
 
 def projected_partial(projected, weights):
-    return jnp.concatenate(
-        [
-            sum(dot_back(part, half[c]) for c, part in enumerate(projected)).astype(BF16)
-            for half in weights
-        ],
-        axis=1,
-    )
+    return [
+        sum(dot_back(part, half[c]) for c, part in enumerate(projected)).astype(BF16)
+        for half in weights
+    ]
 
 
 def body(
@@ -526,16 +556,19 @@
     query_document, local_place = documents(query_place)
     tables = rotary_tables(local_place, width)
     masks = []
+    earlier_tables = None
     for index in range(count):
         key_place = jnp.bitwise_xor(position, index) * rows + inner
-        key_document, ignored = documents(key_place)
+        key_document, key_local_place = documents(key_place)
+        if index == 2 and count == 4:
+            earlier_tables = rotary_tables(key_local_place, width)
         masks.append(
             (key_document[:, None] == query_document[None, :])
             & (key_place[:, None] <= query_place[None, :])
         )
     flags = jnp.stack([jnp.any(mask) for mask in masks]).astype(jnp.int32)
     mask = jnp.where(jnp.concatenate(masks, axis=0), 0.0, NEGATIVE).astype(F32)
-    layout = (tables, mask, flags)
+    layout = (tables, earlier_tables, mask, flags)
 
     def both_layers(array):
         arrived = swap_cores(array)
@@ -558,26 +591,28 @@
         own = after(own, *others)
         return own, swap_cores(own)
 
-    qkv_shards = shard_halves(qkv_weight[0])
-    out_shards = shard_halves(out_weight[0].T[None])
+    attention_shards = shard_halves(jnp.concatenate([qkv_weight[0], out_weight[0].T[None]]))
     gate_up_shards = shard_halves(gate_up_weight[0])
     down_shards = shard_halves(down_weight[0].T[None])
 
     start = take_in(inputs)
     normed_zero, statistics_zero = norm_forward(start.astype(F32), gains[0][0], shifts[0][0])
+    earlier_zero = earlier_chip(normed_zero)
     normed_zero = tp_gather(normed_zero)
-    attention_zero = gather(jnp.concatenate([qkv_shards[0], out_shards[0]], axis=0))
-    attention_zero, normed_zero, layout = lax.optimization_barrier(
-        (attention_zero, normed_zero, layout)
+    if earlier_zero is not None:
+        earlier_zero = tp_gather(earlier_zero)
+    attention_zero = gather(attention_shards[0], start)
+    attention_zero, normed_zero, earlier_zero, layout = lax.optimization_barrier(
+        (attention_zero, normed_zero, earlier_zero, layout)
     )
     feed_zero = gather(jnp.concatenate([gate_up_shards[0], down_shards[0]], axis=0))
-    attention_one = gather(
-        jnp.concatenate([qkv_shards[1], out_shards[1]], axis=0), attention_zero
-    )
+    attention_one = gather(attention_shards[1], attention_zero)
     attention_halves = halves(attention_zero)
     qkv_weights = [[half[:3] for half in attention_halves], None]
     out_weights = [[half[3:] for half in attention_halves], None]
-    queries_zero, key_values_zero = project_forward(normed_zero, qkv_weights[0], biases[0], layout)
+    queries_zero, key_values_zero = project_forward(
+        normed_zero, earlier_zero, qkv_weights[0], biases[0], layout
+    )
     hidden_zero, kept_attention_zero = attention_forward(
         start, queries_zero, key_values_zero, out_weights[0], layout
     )
@@ -593,22 +628,30 @@
     kept_feed_zero = gate_forward(second_zero, gate_up_weights[0])
     middle = down_forward(hidden_zero, kept_feed_zero[2], down_weights[0])
     normed_one, statistics_one = norm_forward(middle.astype(F32), gains[1][0], shifts[1][0])
+    earlier_one = earlier_chip(normed_one)
     normed_one = tp_gather(normed_one)
+    if earlier_one is not None:
+        earlier_one = tp_gather(earlier_one)
     attention_one, normed_one = lax.optimization_barrier((attention_one, normed_one))
     down_one = gather(down_shards[1], attention_one)
     attention_halves = halves(attention_one)
     qkv_weights[1] = [half[:3] for half in attention_halves]
     out_weights[1] = [half[3:] for half in attention_halves]
-    queries_one, key_values_one = project_forward(normed_one, qkv_weights[1], biases[1], layout)
+    queries_one, key_values_one = project_forward(
+        normed_one, earlier_one, qkv_weights[1], biases[1], layout
+    )
     hidden_one, kept_attention_one = attention_forward(
         middle, queries_one, key_values_one, out_weights[1], layout
     )
     second_one, second_statistics_one = norm_forward(hidden_one, gains[1][1], shifts[1][1])
     second_one = tp_gather(second_one)
-    gate_up_one, second_one = lax.optimization_barrier((gate_up_one, second_one))
+    home_zero = send_home(0, after(middle, key_values_one))
+    gate_up_one, second_one, home_zero = lax.optimization_barrier(
+        (gate_up_one, second_one, home_zero)
+    )
+    home_zero = spread_home(0, home_zero)
     gate_up_weights[1] = halves(gate_up_one)
     kept_feed_one = gate_forward(second_one, gate_up_weights[1])
-    home_zero = send_home(0, after(middle, second_one))
 
     kept_feed = (kept_feed_zero, kept_feed_one)
     kept_attention = (kept_attention_zero, kept_attention_one)
@@ -625,7 +668,7 @@
     input_grads = [None, None]
     small_grads = [None, None]
     scattered = [None, None]
-    tables, mask, flags = layout
+    tables, earlier_tables, mask, flags = layout
     for layer in (1, 0):
         down_total = weight_grad(grad_full, [kept_feed[layer][2]])
         if layer == 1:
@@ -644,9 +687,6 @@
         branch_grad = tp_gather(hidden_grad.astype(BF16))
         up_total = weight_grad(second_normed[layer], [up_grad])
         branch_grad, up_total = lax.optimization_barrier((branch_grad, up_total))
-        if layer == 1:
-            branch_grad, home_zero = lax.optimization_barrier((branch_grad, home_zero))
-            home_zero = spread_home(0, home_zero)
         if layer == 0:
             branch_grad = after(branch_grad, attention_grad)
         queries, key_values, attended, attended_low, log_total = kept_attention[layer]
@@ -661,18 +701,17 @@
         query_grad, key_value_grads = after((query_grad, key_value_grads), down_grad)
         gate_weight_grad = scatter_weight_grad(gate_total)
         key_value_grad = after(scatter_chunks(key_value_grads), gate_weight_grad)
-        up_weight_grad = scatter_weight_grad(after(up_total, key_value_grad))
         if layer == 0:
             home_one = send_home(1, after(jnp.concatenate([last, input_grads[1]]), query_grad))
             key_value_grad, home_one = lax.optimization_barrier((key_value_grad, home_one))
-            home_one = spread_home(1, home_one)
         out_total = weight_grad(branch_grad, [attended_low])
         query_grad = rotate(query_grad, tables, -1.0).astype(BF16)
         key_value_grad, out_total, query_grad = lax.optimization_barrier(
             (key_value_grad, out_total, query_grad)
         )
-        if layer == 1:
-            key_value_grad, home_zero = lax.optimization_barrier((key_value_grad, home_zero))
+        up_weight_grad = scatter_weight_grad(
+            after(jnp.concatenate([up_total, out_total], axis=2), key_value_grad)
+        )
         key_grad = rotate(key_value_grad[0], tables, -1.0).astype(BF16)
         projected = (query_grad, key_grad, key_value_grad[1].astype(BF16))
         partial = projected_partial(projected, qkv_weights[layer])
@@ -683,27 +722,27 @@
         moved, gain_first, shift_first = norm_backward(*first_norm[layer], first_grad)
         grad = (hidden_grad + moved).astype(BF16)
         input_grads[layer] = grad
-        attention_total = jnp.concatenate([qkv_total, out_total])
+        attention_total = qkv_total
         if layer == 0:
-            home_grad, home_one, attention_total = lax.optimization_barrier(
-                (send_home(0, grad), home_one, attention_total)
-            )
+            home_grad = send_home(0, grad)
         attention_grad = scatter_weight_grad(attention_total)
         if layer == 1:
             grad_full = after(tp_gather(grad), up_weight_grad)
         norm_grads = unsplit(jnp.stack([gain_first, gain_second, shift_first, shift_second]))
         small_grads[layer] = (norm_grads, bias_grad)
-        gate_up_grad = jnp.concatenate([gate_weight_grad, up_weight_grad])
-        scattered[layer] = (attention_grad, gate_up_grad, down_grad)
-
-    norm_grads, bias_grads = [
-        jnp.stack(parts) for parts in zip(*[after(small, attention_total) for small in small_grads])
-    ]
+        feed_width = gate_weight_grad.shape[2]
+        gate_up_grad = jnp.concatenate([gate_weight_grad, up_weight_grad[:, :, :feed_width]])
+        out_grad = up_weight_grad[:, :, feed_width:]
+        scattered[layer] = (attention_grad, out_grad, gate_up_grad, down_grad)
+
+    norm_grads, bias_grads = [jnp.stack(parts) for parts in zip(*small_grads)]
     norm_rows = norm_grads.size // LANES
     packed = jnp.concatenate(
         [all_sum(norm_grads.reshape(-1, LANES), ("tp",)), bias_grads.reshape(-1, LANES)]
     )
     packed = all_sum(packed, ("section",))
+    home_one = spread_home(1, after(home_one, packed))
+    packed = after(packed, attention_grad)
     packed = packed + sum(exchange(packed, "ctx", k) for k in range(1, count))
     norm_grads = packed[:norm_rows].reshape(norm_grads.shape)
     bias_grads = packed[norm_rows:].reshape(bias_grads.shape)
@@ -729,11 +768,11 @@
         grad_outputs,
         norm_grads[None, :2],
         norm_grads[None, 2:],
-        joined[0][None, :3],
+        joined[0][None],
         bias_grads[None],
-        joined[0][3].T[None],
-        joined[1][None],
-        joined[2][0].T[None],
+        joined[1][0].T[None],
+        joined[2][None],
+        joined[3][0].T[None],
     )
 
 

time: 1270 us -> 1250 us (0.984)
  waiting for transfers between devices: 598 us -> 501 us
  starting transfers between devices: 155 us -> 198 us
  matrix products: 216 us -> 240 us
  other arithmetic: 127 us -> 144 us
    ppermute x54 -> x78, waiting for transfers between devices: 297 us -> 201 us  [exchange(): lax.ppermute(block, axis, [(i, i ^ bit) for i in range(lax.axis_size(axis...]
    ppermute x4, waiting for transfers between devices: 154 us -> 93.4 us  [across(): return [lax.ppermute(block, 'ctx', pairs) for block in blocks]]
    ppermute x54 -> x78, starting transfers between devices: 63.2 us -> 110 us  [exchange(): lax.ppermute(block, axis, [(i, i ^ bit) for i in range(lax.axis_size(axis...]
    ppermute x6, waiting for transfers between devices: 15.9 us -> 41.6 us  [send_home(): lax.ppermute(piece, both, [(seat(i, half), layer * count + i) for i in ra...]
    all_gather x5, waiting for transfers between devices: 96.1 us -> 115 us  [gather(): return lax.all_gather(after(piece, *others), 'ctx', axis=1, tiled=True)]
    dot_general x28 -> x36, matrix products: 86.3 us -> 99.6 us  [dot(): return jnp.dot(left, right, preferred_element_type=F32)]
    unnamed x312 -> x358, local copies, waits for them, and re-layouts: 30.1 us -> 17.2 us
    concatenate x20 -> x36, other arithmetic: 23.9 us -> 27.6 us  [the longest x9 9.85 us: tp_gather(): jnp.concatenate([second, second_near, second_rest])]
  transfers between devices with their start and end apart: 124 -> 149, of which waited for: 57 -> 76; matrix products, arithmetic and copies ran while one was open for 32% -> 36% of each run, Pallas kernels for 4% -> 4%
where the time goes in v1:
time: 1250 us; the launch traced here: 1240 us
  waiting for transfers between devices  501 us (40%)
  matrix products  240 us (19%)
  starting transfers between devices  198 us (16%)
  other arithmetic  144 us (12%)
  local copies, waits for them, and re-layouts  92.4 us (7%)
  Pallas kernels  44.8 us (4%)
  between operations  18.4 us (1%)
    ppermute x78, waiting for transfers between devices, exchange(): lax.ppermute(block, axis, [(i, i ^ bit) for i in range(lax.axis_size(axis...  201 us
    all_gather x5, waiting for transfers between devices, gather(): return lax.all_gather(after(piece, *others), 'ctx', axis=1, tiled=True)  115 us
    ppermute x78, starting transfers between devices, exchange(): lax.ppermute(block, axis, [(i, i ^ bit) for i in range(lax.axis_size(axis...  110 us
    dot_general x36, matrix products, dot(): return jnp.dot(left, right, preferred_element_type=F32)  99.6 us
    ppermute x4, waiting for transfers between devices, across(): return [lax.ppermute(block, 'ctx', pairs) for block in blocks]  93.4 us
    dot_general x28, matrix products, dot_back(): lax.dot_general(left, right, CONTRACT_LAST, preferred_element_type=F32)  70.2 us
    dot_general x28, matrix products, token_sum(): lax.dot_general(left, right, CONTRACT_FIRST, preferred_element_type=F32)  69.7 us
    ppermute x6, waiting for transfers between devices, send_home(): lax.ppermute(piece, both, [(seat(i, half), layer * count + i) for i in ra...  41.6 us
  transfers between devices with their start and end apart: 149, of which 76 were waited for; matrix products, arithmetic and copies ran while one was open for 36% of the time, Pallas kernels for 4%

profile of v1, /device:TPU:0, one launch (start us, length us, event | category | flops | bytes accessed | tf_op | source)
XLA Modules:
  0.0 1238.3 jit_solution(16417074313394036750)
XLA Ops:
  51.2 11.0 collective-permute-done.10
  76.3 8.1 collective-permute-done.14
  86.8 25.1 %all-gather.8.cloned.1.call-done = bf16[4,1024,512]{2,1,0:T(8,128)(2,1)} async-done(((bf16[4,256,512]{2,1,0:T(8,128)(2,1)}), bf16[4,1024,512]{2,1,0:T(8,128)(2,1)}) %all-gather.8.cloned.1.call-update) | async-done | bytes 4194320 | tf_op jit(solution)/shard_map/all_gather | solution.py:588
  171.7 9.4 attend.2
  243.1 7.1 collective-permute-done.31
  252.8 48.9 %all-gather.6.cloned.1.call-done = bf16[3,1024,1408]{2,1,0:T(8,128)(2,1)} async-done(((bf16[3,256,1408]{2,1,0:T(8,128)(2,1)}), bf16[3,1024,1408]{2,1,0:T(8,128)(2,1)}) %all-gather.6.cloned.1.call-update) | async-done | bytes 8650768 | tf_op jit(solution)/shard_map/all_gather | solution.py:588
  319.3 6.5 multiply_convert_fusion.5
  336.9 7.3 collective-permute-done.33
  368.8 7.3 collective-permute-done.40
  384.3 12.4 %collective-permute-done.43 = bf16[128,2048]{1,0:T(8,128)(2,1)S(1)} collective-permute-done((bf16[128,2048]{1,0:T(8,128)(2,1)}, bf16[128,2048]{1,0:T(8,128)(2,1)S(1)}, u32[]{:S(2)}, u32[]{:S(2)}) %collective-permute-start.43) | collective-permute-done | bytes 524320 | tf_op jit(solution)/shard_map/ppermute | solution.py:268
  414.9 7.3 collective-permute-done.45
  444.3 9.4 attend.3
  491.8 16.3 %collective-permute-done.58 = bf16[128,2048]{1,0:T(8,128)(2,1)S(1)} collective-permute-done((bf16[128,2048]{1,0:T(8,128)(2,1)S(1)}, bf16[128,2048]{1,0:T(8,128)(2,1)S(1)}, u32[]{:S(2)}, u32[]{:S(2)}) %collective-permute-start.58) | collective-permute-done | bytes 524320 | tf_op jit(solution)/shard_map/ppermute | solution.py:523
  530.4 6.5 multiply_convert_fusion.4
  547.6 30.2 %all-gather.14.cloned.1.call-done = bf16[1,1024,1408]{2,1,0:T(8,128)(2,1)} async-done(((bf16[1,256,1408]{2,1,0:T(8,128)(2,1)}), bf16[1,1024,1408]{2,1,0:T(8,128)(2,1)}) %all-gather.14.cloned.1.call-update) | async-done | bytes 2883600 | tf_op jit(solution)/shard_map/all_gather | solution.py:588
  655.8 12.8 %attend_back.2 = (f32[512,512]{1,0:T(8,128)S(1)}, bf16[2,512,512]{2,1,0:T(8,128)(2,1)S(1)}, bf16[2,512,512]{2,1,0:T(8,128)(2,1)S(1)}, bf16[2,512,512]{2,1,0:T(8,128)(2,1)S(1)}, bf16[2,512,512]{2,1,0:T(8,128)(2,1)}) custom-call(s32[4]{0:T(128)S(1)} %add_convert_fusion.12.refs_0_, bf16[512,512]{1,0:T(8,128)(2,1)S(1)} %copy-done.7, ...), custom_call_target="tpu_custom_call" | custom-call | flops 10737418240 | bytes 12582912 | tf_op jit(solution)/shard_map/attend_back/pallas_call | solution.py:181
  680.4 34.1 %collective-permute-done.74 = bf16[2,512,512]{2,1,0:T(8,128)(2,1)S(1)} collective-permute-done((bf16[2,512,512]{2,1,0:T(8,128)(2,1)S(1)}, bf16[2,512,512]{2,1,0:T(8,128)(2,1)S(1)}, u32[]{:S(2)}, u32[]{:S(2)}) %collective-permute-start.74) | collective-permute-done | bytes 1048608 | tf_op jit(solution)/shard_map/ppermute | solution.py:268
  904.0 13.2 %attend_back.3 = (f32[512,512]{1,0:T(8,128)S(1)}, bf16[2,512,512]{2,1,0:T(8,128)(2,1)S(1)}, bf16[2,512,512]{2,1,0:T(8,128)(2,1)S(1)}, bf16[2,512,512]{2,1,0:T(8,128)(2,1)S(1)}, bf16[2,512,512]{2,1,0:T(8,128)(2,1)}) custom-call(s32[4]{0:T(128)S(1)} %add_convert_fusion.12.refs_0_, bf16[512,512]{1,0:T(8,128)(2,1)S(1)} %copy-done.5, ...), custom_call_target="tpu_custom_call" | custom-call | flops 10737418240 | bytes 12582912 | tf_op jit(solution)/shard_map/attend_back/pallas_call | solution.py:181
  946.5 13.9 %collective-permute-start.96 = (bf16[2,512,512]{2,1,0:T(8,128)(2,1)}, bf16[2,512,512]{2,1,0:T(8,128)(2,1)S(1)}, u32[]{:S(2)}, u32[]{:S(2)}) collective-permute-start(bf16[2,512,512]{2,1,0:T(8,128)(2,1)} %copy-done.10), channel_id=1, source_target_pairs={{0,16},{16,0},{1,17},{17,1},{2,18},{18,2},{3,19},{19,3},{4,20},{20... | collective-permute-start | bytes 3145736 | tf_op jit(solution)/shard_map/ppermute | solution.py:211
  971.0 35.9 %collective-permute-done.98 = bf16[2,512,512]{2,1,0:T(8,128)(2,1)S(1)} collective-permute-done((bf16[2,512,512]{2,1,0:T(8,128)(2,1)S(1)}, bf16[2,512,512]{2,1,0:T(8,128)(2,1)S(1)}, u32[]{:S(2)}, u32[]{:S(2)}) %collective-permute-start.98) | collective-permute-done | bytes 1048608 | tf_op jit(solution)/shard_map/ppermute | solution.py:268
  1050.1 9.7 collective-permute-done.108
  1095.1 25.3 %collective-permute-done.121 = bf16[128,2048]{1,0:T(8,128)(2,1)} collective-permute-done((bf16[128,2048]{1,0:T(8,128)(2,1)}, bf16[128,2048]{1,0:T(8,128)(2,1)}, u32[]{:S(2)}, u32[]{:S(2)}) %collective-permute-start.121) | collective-permute-done | bytes 524320 | tf_op jit(solution)/shard_map/ppermute | solution.py:523
  1164.3 11.3 collective-permute-done.124
  1210.5 8.7 collective-permute-start.125
  (1110 shorter events, 842.2 us)
Async XLA Ops:
  7.2 104.8 %all-gather.8.cloned.1.call-start = ((), (), s32[]{:S(2)}) async-start(), calls=%async_computation.9 | async-start | bytes 5242880 | tf_op jit(solution)/shard_map/all_gather | solution.py:588
  25.6 276.1 %all-gather.6.cloned.1.call-start = ((), (), s32[]{:S(2)}) async-start(), calls=%async_computation.8 | async-start | bytes 10813440 | tf_op jit(solution)/shard_map/all_gather | solution.py:588
  134.2 248.8 %all-gather.12.cloned.1.call-start = ((), (), s32[]{:S(2)}) async-start(), calls=%async_computation.11 | async-start | bytes 5242880 | tf_op jit(solution)/shard_map/all_gather | solution.py:588
  302.1 214.6 %all-gather.10.cloned.1.call-start = ((), (), s32[]{:S(2)}) async-start(), calls=%async_computation.10 | async-start | bytes 7208960 | tf_op jit(solution)/shard_map/all_gather | solution.py:588
  383.0 39.3 %collective-permute-start.41 = (bf16[4,1024,512]{2,1,0:T(8,128)(2,1)}, bf16[4,1024,512]{2,1,0:T(8,128)(2,1)}, u32[]{:S(2)}, u32[]{:S(2)}) collective-permute-start(bf16[4,1024,512]{2,1,0:T(8,128)(2,1)} %all-gather.12.cloned.1.call-done), channel_id=1, source_target_pairs={{0,16},{16,0},{1,17},{17,1},{2,18},{18,2},{3,19},{19,3},{4,20},{20... | collective-permute-start | bytes 12582920 | tf_op jit(solution)/shard_map/ppermute | solution.py:211
  400.6 177.3 %all-gather.14.cloned.1.call-start = ((), (), s32[]{:S(2)}) async-start(), calls=%async_computation.12 | async-start | bytes 3604480 | tf_op jit(solution)/shard_map/all_gather | solution.py:588
  516.9 152.7 %reduce-scatter.9.cloned.1.call-start = ((), (), s32[]{:S(2)}) async-start(), calls=%async_computation.13 | async-start | bytes 3604480 | tf_op jit(solution)/shard_map/reduce_scatter | solution.py:430
  577.9 138.4 %reduce-scatter.11.cloned.1.call-start = ((), (), s32[]{:S(2)}) async-start(), calls=%async_computation.14 | async-start | bytes 3604480 | tf_op jit(solution)/shard_map/reduce_scatter | solution.py:430
  634.3 159.3 %reduce-scatter.13.cloned.1.call-start = ((), (), s32[]{:S(2)}) async-start(), calls=%async_computation.15 | async-start | bytes 4915200 | tf_op jit(solution)/shard_map/reduce_scatter | solution.py:430
  675.6 38.8 %collective-permute-start.74 = (bf16[2,512,512]{2,1,0:T(8,128)(2,1)S(1)}, bf16[2,512,512]{2,1,0:T(8,128)(2,1)S(1)}, u32[]{:S(2)}, u32[]{:S(2)}) collective-permute-start(bf16[2,512,512]{2,1,0:T(8,128)(2,1)S(1)} %add_convert_fusion.7), channel_id=1, source_target_pairs={{4,0},{8,12},{5,1},{9,13},{6,2},{10,14},{7,3},{11,15},{20,16},{24,... | collective-permute-start | bytes 3145736 | tf_op jit(solution)/shard_map/ppermute | solution.py:268
  720.3 164.2 %reduce-scatter.15.cloned.1.call-start = ((), (), s32[]{:S(2)}) async-start(), calls=%async_computation.16 | async-start | bytes 3932160 | tf_op jit(solution)/shard_map/reduce_scatter | solution.py:430
  764.8 163.6 %reduce-scatter.17.cloned.1.call-start = ((), (), s32[]{:S(2)}) async-start(), calls=%async_computation.17 | async-start | bytes 3604480 | tf_op jit(solution)/shard_map/reduce_scatter | solution.py:430
  777.7 188.2 %collective-permute-start.134 = (bf16[1,256,1408]{2,1,0:T(8,128)(2,1)}, bf16[1,256,1408]{2,1,0:T(8,128)(2,1)}, u32[]{:S(2)}, u32[]{:S(2)}) collective-permute-start(bf16[1,256,1408]{2,1,0:T(8,128)(2,1)} %reduce-scatter.9.cloned.1.call-done), channel_id=1, source_target_pairs={{0,16},{1,17},{2,18},{3,19},{4,20},{5,21},{6,22},{7,23},{8,24},{9,... | collective-permute-start | bytes 2162696 | tf_op jit(solution)/shard_map/ppermute | solution.py:760
  811.7 46.8 %collective-permute-start.89 = (bf16[1,1024,1408]{2,1,0:T(8,128)(2,1)}, bf16[1,1024,1408]{2,1,0:T(8,128)(2,1)}, u32[]{:S(2)}, u32[]{:S(2)}) collective-permute-start(bf16[1,1024,1408]{2,1,0:T(8,128)(2,1)} %fusion.11), channel_id=1, source_target_pairs={{0,16},{16,0},{1,17},{17,1},{2,18},{18,2},{3,19},{19,3},{4,20},{20... | collective-permute-start | bytes 8650760 | tf_op jit(solution)/shard_map/ppermute | solution.py:211
  822.3 186.3 %reduce-scatter.19.cloned.1.call-start = ((), (), s32[]{:S(2)}) async-start(), calls=%async_computation.18 | async-start | bytes 3604480 | tf_op jit(solution)/shard_map/reduce_scatter | solution.py:430
  871.5 315.1 %reduce-scatter.23.cloned.1.call-start = ((), (), s32[]{:S(2)}) async-start(), calls=%async_computation.20 | async-start | bytes 4915200 | tf_op jit(solution)/shard_map/reduce_scatter | solution.py:430
  962.0 44.9 %collective-permute-start.98 = (bf16[2,512,512]{2,1,0:T(8,128)(2,1)S(1)}, bf16[2,512,512]{2,1,0:T(8,128)(2,1)S(1)}, u32[]{:S(2)}, u32[]{:S(2)}) collective-permute-start(bf16[2,512,512]{2,1,0:T(8,128)(2,1)S(1)} %add_convert_fusion.2), channel_id=1, source_target_pairs={{4,0},{8,12},{5,1},{9,13},{6,2},{10,14},{7,3},{11,15},{20,16},{24,... | collective-permute-start | bytes 3145736 | tf_op jit(solution)/shard_map/ppermute | solution.py:268
  966.0 121.6 %collective-permute-start.135 = (bf16[1,256,1408]{2,1,0:T(8,128)(2,1)}, bf16[1,256,1408]{2,1,0:T(8,128)(2,1)}, u32[]{:S(2)}, u32[]{:S(2)}) collective-permute-start(bf16[1,256,1408]{2,1,0:T(8,128)(2,1)} %reduce-scatter.17.cloned.1.call-done), channel_id=1, source_target_pairs={{16,0},{17,1},{18,2},{19,3},{20,4},{21,5},{22,6},{23,7},{24,8},{25... | collective-permute-start | bytes 2162696 | tf_op jit(solution)/shard_map/ppermute | solution.py:759
  1025.2 185.4 %reduce-scatter.21.cloned.1.call-start = ((), (), s32[]{:S(2)}) async-start(), calls=%async_computation.19 | async-start | bytes 3932160 | tf_op jit(solution)/shard_map/reduce_scatter | solution.py:430
  1085.5 63.7 %collective-permute-start.115 = (bf16[2,256,2048]{2,1,0:T(8,128)(2,1)}, bf16[2,256,2048]{2,1,0:T(8,128)(2,1)}, u32[]{:S(2)}, u32[]{:S(2)}) collective-permute-start(bf16[2,256,2048]{2,1,0:T(8,128)(2,1)} %pad_maximum_fusion.5), channel_id=1, source_target_pairs={{16,17},{17,16},{18,19},{19,18},{20,21},{21,20},{22,23},{23,22},{2... | collective-permute-start | bytes 6291464 | tf_op jit(solution)/shard_map/ppermute | solution.py:532
  1088.7 70.2 %collective-permute-start.117 = (bf16[2,256,2048]{2,1,0:T(8,128)(2,1)}, bf16[2,256,2048]{2,1,0:T(8,128)(2,1)}, u32[]{:S(2)}, u32[]{:S(2)}) collective-permute-start(bf16[2,256,2048]{2,1,0:T(8,128)(2,1)} %pad_maximum_fusion.5), channel_id=1, source_target_pairs={{16,18},{17,19},{18,16},{19,17},{20,22},{21,23},{22,20},{23,21},{2... | collective-permute-start | bytes 6291464 | tf_op jit(solution)/shard_map/ppermute | solution.py:532
  1094.3 83.8 %collective-permute-start.119 = (bf16[2,256,2048]{2,1,0:T(8,128)(2,1)}, bf16[2,256,2048]{2,1,0:T(8,128)(2,1)S(1)}, u32[]{:S(2)}, u32[]{:S(2)}) collective-permute-start(bf16[2,256,2048]{2,1,0:T(8,128)(2,1)} %pad_maximum_fusion.5), channel_id=1, source_target_pairs={{16,19},{17,18},{18,17},{19,16},{20,23},{21,22},{22,21},{23,20},{2... | collective-permute-start | bytes 6291464 | tf_op jit(solution)/shard_map/ppermute | solution.py:532
  1156.4 39.3 %collective-permute-start.116 = (bf16[2,128,2048]{2,1,0:T(8,128)(2,1)S(1)}, bf16[2,128,2048]{2,1,0:T(8,128)(2,1)}, u32[]{:S(2)}, u32[]{:S(2)}) collective-permute-start(bf16[2,128,2048]{2,1,0:T(8,128)(2,1)S(1)} %copy-done.69), channel_id=1, source_target_pairs={{0,2},{1,3},{2,0},{3,1},{4,6},{5,7},{6,4},{7,5},{8,10},{9,11},{10,... | collective-permute-start | bytes 3145736 | tf_op jit(solution)/shard_map/ppermute | solution.py:532
  1181.8 41.1 %collective-permute-start.128 = (bf16[3,256,512]{2,1,0:T(8,128)(2,1)}, bf16[3,256,512]{2,1,0:T(8,128)(2,1)}, u32[]{:S(2)}, u32[]{:S(2)}) collective-permute-start(bf16[3,256,512]{2,1,0:T(8,128)(2,1)} %reduce-scatter.15.cloned.1.call-done), channel_id=1, source_target_pairs={{0,16},{1,17},{2,18},{3,19},{4,20},{5,21},{6,22},{7,23},{8,24},{9,... | collective-permute-start | bytes 2359304 | tf_op jit(solution)/shard_map/ppermute | solution.py:760
  (295 other events, 4356.4 us)
Sparse Core Ops, SparseCore 0:
  25.7 86.1 all-gather.7
  134.3 167.4 all-gather.5
  303.9 79.0 all-gather.11
  400.7 116.0 all-gather.9
  518.2 59.5 all-gather.13
  580.0 54.8 reduce-scatter.8
  637.8 56.5 reduce-scatter.10
  720.4 73.0 reduce-scatter.12
  796.4 60.6 reduce-scatter.14
  859.8 56.1 reduce-scatter.16
  918.9 64.5 reduce-scatter.18
  1025.3 88.4 reduce-scatter.22
  1116.7 64.3 reduce-scatter.20

commit v2 on v1

--- a/solution.py
+++ b/solution.py
@@ -389,12 +389,12 @@
         )
 
     own = key_value(normed, tables)
+    queries = rotate(project(normed, 0), tables, 1.0).astype(BF16)
     if earlier is None:
-        key_values = gather_chunks(own)
-    else:
-        blocks = [own, key_value(earlier, earlier_tables)]
-        key_values = [each for block in blocks for each in (block, swap_cores(block))]
-    return rotate(project(normed, 0), tables, 1.0).astype(BF16), key_values
+        return queries, gather_chunks(own)
+    own, queries, earlier = lax.optimization_barrier((own, queries, earlier))
+    blocks = [own, key_value(tp_gather(earlier), earlier_tables)]
+    return queries, [each for block in blocks for each in (block, swap_cores(block))]
 
 
 def attention_forward(piece, queries, key_values, out_weights, layout):
@@ -525,12 +525,25 @@
             ]
         )
 
-    def spread_home(layer, own):
-        blocks = [own]
-        for k in range(1, ranks):
+    def spread_home(layer, own, steps=2):
+        def send(block, k):
             pairs = [(layer * ranks + i, layer * ranks + (i ^ k)) for i in range(ranks)]
-            blocks.append(lax.ppermute(own, ("section", "tp"), pairs))
-        return blocks
+            return lax.ppermute(block, ("section", "tp"), pairs)
+
+        if ranks != 4 or steps == 1:
+            return [own] + [send(own, k) for k in range(1, ranks)]
+        middle = features // 2
+        first, second = own[..., :middle], own[..., middle:]
+        first_far, second_near = send(first, 2), send(second, 1)
+        first_rest = send(jnp.stack([first, first_far]), 1)
+        second_rest = send(jnp.stack([second, second_near]), 2)
+        return [
+            jnp.concatenate(pair, axis=-1)
+            for pair in zip(
+                (first, first_rest[0], first_far, first_rest[1]),
+                (second, second_near, second_rest[0], second_rest[1]),
+            )
+        ]
 
     def assemble(blocks, dtype):
         whole = jnp.zeros((2, rows, features), dtype)
@@ -598,15 +611,17 @@
     start = take_in(inputs)
     normed_zero, statistics_zero = norm_forward(start.astype(F32), gains[0][0], shifts[0][0])
     earlier_zero = earlier_chip(normed_zero)
+    feed_shards = jnp.concatenate([gate_up_shards[0], down_shards[0]], axis=0)
+    normed_zero, feed_shards, layout = lax.optimization_barrier(
+        (normed_zero, feed_shards, layout)
+    )
     normed_zero = tp_gather(normed_zero)
-    if earlier_zero is not None:
-        earlier_zero = tp_gather(earlier_zero)
-    attention_zero = gather(attention_shards[0], start)
-    attention_zero, normed_zero, earlier_zero, layout = lax.optimization_barrier(
-        (attention_zero, normed_zero, earlier_zero, layout)
-    )
-    feed_zero = gather(jnp.concatenate([gate_up_shards[0], down_shards[0]], axis=0))
-    attention_one = gather(attention_shards[1], attention_zero)
+    attention_zero = gather(attention_shards[0])
+    grad = take_in(after(cotangent, start))
+    attention_zero, normed_zero, earlier_zero, layout, grad = lax.optimization_barrier(
+        (attention_zero, normed_zero, earlier_zero, layout, grad)
+    )
+    feed_zero = gather(feed_shards)
     attention_halves = halves(attention_zero)
     qkv_weights = [[half[:3] for half in attention_halves], None]
     out_weights = [[half[3:] for half in attention_halves], None]
@@ -617,11 +632,16 @@
         start, queries_zero, key_values_zero, out_weights[0], layout
     )
     second_zero, second_statistics_zero = norm_forward(hidden_zero, gains[0][1], shifts[0][1])
+    second_zero, attention_shard_one, gate_up_shard_one, down_shard_one = (
+        lax.optimization_barrier(
+            (second_zero, attention_shards[1], gate_up_shards[1], down_shards[1])
+        )
+    )
+    attention_one = gather(attention_shard_one, attention_zero)
     second_zero = tp_gather(second_zero)
-    grad = take_in(after(cotangent, normed_zero))
-    grad_full = tp_gather(after(grad, second_zero))
+    grad_full = tp_gather(after(grad, hidden_zero))
     feed_zero, second_zero, grad_full = lax.optimization_barrier((feed_zero, second_zero, grad_full))
-    gate_up_one = gather(gate_up_shards[1], feed_zero)
+    gate_up_one = gather(gate_up_shard_one, feed_zero)
     feed_halves = halves(feed_zero)
     gate_up_weights = [[half[:2] for half in feed_halves], None]
     down_weights = [[half[2:] for half in feed_halves], None]
@@ -630,10 +650,8 @@
     normed_one, statistics_one = norm_forward(middle.astype(F32), gains[1][0], shifts[1][0])
     earlier_one = earlier_chip(normed_one)
     normed_one = tp_gather(normed_one)
-    if earlier_one is not None:
-        earlier_one = tp_gather(earlier_one)
     attention_one, normed_one = lax.optimization_barrier((attention_one, normed_one))
-    down_one = gather(down_shards[1], attention_one)
+    down_one = gather(down_shard_one, attention_one)
     attention_halves = halves(attention_one)
     qkv_weights[1] = [half[:3] for half in attention_halves]
     out_weights[1] = [half[3:] for half in attention_halves]
@@ -644,12 +662,11 @@
         middle, queries_one, key_values_one, out_weights[1], layout
     )
     second_one, second_statistics_one = norm_forward(hidden_one, gains[1][1], shifts[1][1])
+    home_zero = send_home(0, after(middle, key_values_one))
+    gate_up_one, second_one = lax.optimization_barrier((gate_up_one, second_one))
     second_one = tp_gather(second_one)
-    home_zero = send_home(0, after(middle, key_values_one))
-    gate_up_one, second_one, home_zero = lax.optimization_barrier(
-        (gate_up_one, second_one, home_zero)
-    )
-    home_zero = spread_home(0, home_zero)
+    second_one, home_zero = lax.optimization_barrier((second_one, home_zero))
+    home_zero = spread_home(0, home_zero, steps=1)
     gate_up_weights[1] = halves(gate_up_one)
     kept_feed_one = gate_forward(second_one, gate_up_weights[1])
 
@@ -672,8 +689,8 @@
     for layer in (1, 0):
         down_total = weight_grad(grad_full, [kept_feed[layer][2]])
         if layer == 1:
-            down_one, down_total, grad_full = lax.optimization_barrier(
-                (down_one, down_total, grad_full)
+            down_one, down_total, grad_full, home_zero = lax.optimization_barrier(
+                (down_one, down_total, grad_full, home_zero)
             )
             down_weights[1] = halves(down_one)
         gate_grad, up_grad = gate_backward(grad_full, kept_feed[layer], down_weights[layer])
@@ -737,11 +754,10 @@
 
     norm_grads, bias_grads = [jnp.stack(parts) for parts in zip(*small_grads)]
     norm_rows = norm_grads.size // LANES
-    packed = jnp.concatenate(
-        [all_sum(norm_grads.reshape(-1, LANES), ("tp",)), bias_grads.reshape(-1, LANES)]
-    )
+    norm_grads_sum = all_sum(norm_grads.reshape(-1, LANES), ("tp",))
+    home_one = spread_home(1, after(home_one, norm_grads_sum))
+    packed = jnp.concatenate([norm_grads_sum, bias_grads.reshape(-1, LANES)])
     packed = all_sum(packed, ("section",))
-    home_one = spread_home(1, after(home_one, packed))
     packed = after(packed, attention_grad)
     packed = packed + sum(exchange(packed, "ctx", k) for k in range(1, count))
     norm_grads = packed[:norm_rows].reshape(norm_grads.shape)

time: 1250 us -> 1220 us (0.976)
  waiting for transfers between devices: 501 us -> 469 us
  matrix products: 240 us -> 226 us
  local copies, waits for them, and re-layouts: 92.4 us -> 105 us
    all_gather x5, waiting for transfers between devices: 115 us -> 96.1 us  [gather(): return lax.all_gather(after(piece, *others), 'ctx', axis=1, tiled=True)]
    ppermute x78, waiting for transfers between devices: 201 us -> 217 us  [exchange(): lax.ppermute(block, axis, [(i, i ^ bit) for i in range(lax.axis_size(axis...]
    ppermute x4, waiting for transfers between devices: 93.4 us -> 77.4 us  [across(): return [lax.ppermute(block, 'ctx', pairs) for block in blocks]]
    unnamed x358 -> x412, local copies, waits for them, and re-layouts: 17.2 us -> 27.6 us
    ppermute x9 -> x11, starting transfers between devices: 23.7 us -> 26.7 us  [send(): return lax.ppermute(block, ('section', 'tp'), pairs)]
  transfers between devices with their start and end apart: 149 -> 151, of which waited for: 76 -> 78; matrix products, arithmetic and copies ran while one was open for 36% -> 37% of each run, Pallas kernels for 4% -> 4%
where the time goes in v2:
time: 1220 us; the launch traced here: 1210 us
  waiting for transfers between devices  469 us (38%)
  matrix products  226 us (19%)
  starting transfers between devices  199 us (16%)
  other arithmetic  148 us (12%)
  local copies, waits for them, and re-layouts  105 us (9%)
  Pallas kernels  44.9 us (4%)
  between operations  18.6 us (2%)
    ppermute x78, waiting for transfers between devices, exchange(): lax.ppermute(block, axis, [(i, i ^ bit) for i in range(lax.axis_size(axis...  217 us
    ppermute x78, starting transfers between devices, exchange(): lax.ppermute(block, axis, [(i, i ^ bit) for i in range(lax.axis_size(axis...  108 us
    all_gather x5, waiting for transfers between devices, gather(): return lax.all_gather(after(piece, *others), 'ctx', axis=1, tiled=True)  96.1 us
    dot_general x36, matrix products, dot(): return jnp.dot(left, right, preferred_element_type=F32)  93.9 us
    ppermute x4, waiting for transfers between devices, across(): return [lax.ppermute(block, 'ctx', pairs) for block in blocks]  77.4 us
    dot_general x28, matrix products, dot_back(): lax.dot_general(left, right, CONTRACT_LAST, preferred_element_type=F32)  67.3 us
    dot_general x28, matrix products, token_sum(): lax.dot_general(left, right, CONTRACT_FIRST, preferred_element_type=F32)  64.8 us
    ppermute x6, waiting for transfers between devices, send_home(): lax.ppermute(piece, both, [(seat(i, half), layer * count + i) for i in ra...  32 us
  transfers between devices with their start and end apart: 151, of which 78 were waited for; matrix products, arithmetic and copies ran while one was open for 37% of the time, Pallas kernels for 4%

profile of v2, /device:TPU:0, one launch (start us, length us, event | category | flops | bytes accessed | tf_op | source)
XLA Modules:
  0.0 1210.7 jit_solution(2081851862348379162)
XLA Ops:
  93.8 9.9 collective-permute-done.10
  103.7 23.6 %all-gather.6.cloned.1.call-done = bf16[4,1024,512]{2,1,0:T(8,128)(2,1)} async-done(((bf16[4,256,512]{2,1,0:T(8,128)(2,1)}), bf16[4,1024,512]{2,1,0:T(8,128)(2,1)}) %all-gather.6.cloned.1.call-update) | async-done | bytes 4194320 | tf_op jit(solution)/shard_map/all_gather | solution.py:601
  192.1 9.4 attend.2
  238.2 14.6 %collective-permute-done.24 = bf16[128,1024]{1,0:T(8,128)(2,1)S(1)} collective-permute-done((bf16[128,1024]{1,0:T(8,128)(2,1)S(1)}, bf16[128,1024]{1,0:T(8,128)(2,1)S(1)}, u32[]{:S(2)}, u32[]{:S(2)}) %collective-permute-start.24) | collective-permute-done | bytes 262176 | tf_op jit(solution)/shard_map/ppermute | solution.py:215
  256.6 7.4 collective-permute-done.27
  267.3 22.5 %all-gather.10.cloned.1.call-done = bf16[3,1024,1408]{2,1,0:T(8,128)(2,1)} async-done(((bf16[3,256,1408]{2,1,0:T(8,128)(2,1)}), bf16[3,1024,1408]{2,1,0:T(8,128)(2,1)}) %all-gather.10.cloned.1.call-update) | async-done | bytes 8650768 | tf_op jit(solution)/shard_map/all_gather | solution.py:601
  307.4 6.5 multiply_convert_fusion.5
  324.9 7.3 collective-permute-done.33
  356.9 7.3 collective-permute-done.40
  399.1 9.8 collective-permute-done.45
  421.6 9.4 attend.3
  436.2 6.8 collective-permute-done.49
  453.8 24.4 %all-gather.14.cloned.1.call-done = bf16[2,1024,1408]{2,1,0:T(8,128)(2,1)} async-done(((bf16[2,256,1408]{2,1,0:T(8,128)(2,1)}), bf16[2,1024,1408]{2,1,0:T(8,128)(2,1)}) %all-gather.14.cloned.1.call-update) | async-done | bytes 5767184 | tf_op jit(solution)/shard_map/all_gather | solution.py:601
  517.4 6.5 multiply_convert_fusion.4
  539.5 20.0 %all-gather.12.cloned.1.call-done = bf16[1,1024,1408]{2,1,0:T(8,128)(2,1)} async-done(((bf16[1,256,1408]{2,1,0:T(8,128)(2,1)}), bf16[1,1024,1408]{2,1,0:T(8,128)(2,1)}) %all-gather.12.cloned.1.call-update) | async-done | bytes 2883600 | tf_op jit(solution)/shard_map/all_gather | solution.py:601
  640.4 12.8 %attend_back.2 = (f32[512,512]{1,0:T(8,128)S(1)}, bf16[2,512,512]{2,1,0:T(8,128)(2,1)S(1)}, bf16[2,512,512]{2,1,0:T(8,128)(2,1)S(1)}, bf16[2,512,512]{2,1,0:T(8,128)(2,1)S(1)}, bf16[2,512,512]{2,1,0:T(8,128)(2,1)}) custom-call(s32[4]{0:T(128)S(1)} %add_convert_fusion.12.refs_0_, bf16[512,512]{1,0:T(8,128)(2,1)S(1)} %copy-done.7, ...), custom_call_target="tpu_custom_call" | custom-call | flops 10737418240 | bytes 12582912 | tf_op jit(solution)/shard_map/attend_back/pallas_call | solution.py:181
  666.3 30.9 %collective-permute-done.77 = bf16[2,512,512]{2,1,0:T(8,128)(2,1)S(1)} collective-permute-done((bf16[2,512,512]{2,1,0:T(8,128)(2,1)S(1)}, bf16[2,512,512]{2,1,0:T(8,128)(2,1)S(1)}, u32[]{:S(2)}, u32[]{:S(2)}) %collective-permute-start.77) | collective-permute-done | bytes 1048608 | tf_op jit(solution)/shard_map/ppermute | solution.py:268
  732.5 6.7 collective-permute-done.81
  770.9 7.4 reduce-scatter.13.cloned.1.call-done
  890.5 13.2 %attend_back.3 = (f32[512,512]{1,0:T(8,128)S(1)}, bf16[2,512,512]{2,1,0:T(8,128)(2,1)S(1)}, bf16[2,512,512]{2,1,0:T(8,128)(2,1)S(1)}, bf16[2,512,512]{2,1,0:T(8,128)(2,1)S(1)}, bf16[2,512,512]{2,1,0:T(8,128)(2,1)}) custom-call(s32[4]{0:T(128)S(1)} %add_convert_fusion.12.refs_0_, bf16[512,512]{1,0:T(8,128)(2,1)S(1)} %copy-done.5, ...), custom_call_target="tpu_custom_call" | custom-call | flops 10737418240 | bytes 12582912 | tf_op jit(solution)/shard_map/attend_back/pallas_call | solution.py:181
  932.5 13.4 %collective-permute-start.99 = (bf16[2,512,512]{2,1,0:T(8,128)(2,1)}, bf16[2,512,512]{2,1,0:T(8,128)(2,1)S(1)}, u32[]{:S(2)}, u32[]{:S(2)}) collective-permute-start(bf16[2,512,512]{2,1,0:T(8,128)(2,1)} %copy-done.10), channel_id=1, source_target_pairs={{0,16},{16,0},{1,17},{17,1},{2,18},{18,2},{3,19},{19,3},{4,20},{20... | collective-permute-start | bytes 3145736 | tf_op jit(solution)/shard_map/ppermute | solution.py:211
  955.8 35.7 %collective-permute-done.101 = bf16[2,512,512]{2,1,0:T(8,128)(2,1)S(1)} collective-permute-done((bf16[2,512,512]{2,1,0:T(8,128)(2,1)S(1)}, bf16[2,512,512]{2,1,0:T(8,128)(2,1)S(1)}, u32[]{:S(2)}, u32[]{:S(2)}) %collective-permute-start.101) | collective-permute-done | bytes 1048608 | tf_op jit(solution)/shard_map/ppermute | solution.py:268
  1072.8 27.8 %collective-permute-done.121 = bf16[128,2048]{1,0:T(8,128)(2,1)S(1)} collective-permute-done((bf16[128,2048]{1,0:T(8,128)(2,1)}, bf16[128,2048]{1,0:T(8,128)(2,1)S(1)}, u32[]{:S(2)}, u32[]{:S(2)}) %collective-permute-start.121) | collective-permute-done | bytes 524320 | tf_op jit(solution)/shard_map/ppermute | solution.py:523
  1142.2 10.4 collective-permute-done.123
  (1175 shorter events, 848.2 us)
Async XLA Ops:
  7.2 120.2 %all-gather.6.cloned.1.call-start = ((), (), s32[]{:S(2)}) async-start(), calls=%async_computation.8 | async-start | bytes 5242880 | tf_op jit(solution)/shard_map/all_gather | solution.py:601
  10.0 37.0 %collective-permute-start.11 = (bf16[128,2048]{1,0:T(8,128)(2,1)}, bf16[128,2048]{1,0:T(8,128)(2,1)}, u32[]{:S(2)}, u32[]{:S(2)}) collective-permute-start(bf16[128,2048]{1,0:T(8,128)(2,1)} %dynamic-slice_bitcast_fusion.1), channel_id=1, source_target_pairs={{0,0},{4,16},{8,4},{12,20},{16,12},{20,28},{24,8},{28,24},{1,1},{5... | collective-permute-start | bytes 1572872 | tf_op jit(solution)/shard_map/ppermute | solution.py:517
  39.7 250.2 %all-gather.10.cloned.1.call-start = ((), (), s32[]{:S(2)}) async-start(), calls=%async_computation.10 | async-start | bytes 10813440 | tf_op jit(solution)/shard_map/all_gather | solution.py:601
  133.3 237.7 %all-gather.8.cloned.1.call-start = ((), (), s32[]{:S(2)}) async-start(), calls=%async_computation.9 | async-start | bytes 5242880 | tf_op jit(solution)/shard_map/all_gather | solution.py:601
  290.3 188.0 %all-gather.14.cloned.1.call-start = ((), (), s32[]{:S(2)}) async-start(), calls=%async_computation.12 | async-start | bytes 7208960 | tf_op jit(solution)/shard_map/all_gather | solution.py:601
  371.0 188.5 %all-gather.12.cloned.1.call-start = ((), (), s32[]{:S(2)}) async-start(), calls=%async_computation.11 | async-start | bytes 3604480 | tf_op jit(solution)/shard_map/all_gather | solution.py:601
  493.4 160.8 %reduce-scatter.9.cloned.1.call-start = ((), (), s32[]{:S(2)}) async-start(), calls=%async_computation.13 | async-start | bytes 3604480 | tf_op jit(solution)/shard_map/reduce_scatter | solution.py:430
  559.6 139.3 %reduce-scatter.11.cloned.1.call-start = ((), (), s32[]{:S(2)}) async-start(), calls=%async_computation.14 | async-start | bytes 3604480 | tf_op jit(solution)/shard_map/reduce_scatter | solution.py:430
  619.5 158.8 %reduce-scatter.13.cloned.1.call-start = ((), (), s32[]{:S(2)}) async-start(), calls=%async_computation.15 | async-start | bytes 4915200 | tf_op jit(solution)/shard_map/reduce_scatter | solution.py:430
  660.3 36.8 %collective-permute-start.77 = (bf16[2,512,512]{2,1,0:T(8,128)(2,1)S(1)}, bf16[2,512,512]{2,1,0:T(8,128)(2,1)S(1)}, u32[]{:S(2)}, u32[]{:S(2)}) collective-permute-start(bf16[2,512,512]{2,1,0:T(8,128)(2,1)S(1)} %add_convert_fusion.7), channel_id=1, source_target_pairs={{4,0},{8,12},{5,1},{9,13},{6,2},{10,14},{7,3},{11,15},{20,16},{24,... | collective-permute-start | bytes 3145736 | tf_op jit(solution)/shard_map/ppermute | solution.py:268
  703.0 167.3 %reduce-scatter.15.cloned.1.call-start = ((), (), s32[]{:S(2)}) async-start(), calls=%async_computation.16 | async-start | bytes 3932160 | tf_op jit(solution)/shard_map/reduce_scatter | solution.py:430
  748.9 165.4 %reduce-scatter.17.cloned.1.call-start = ((), (), s32[]{:S(2)}) async-start(), calls=%async_computation.17 | async-start | bytes 3604480 | tf_op jit(solution)/shard_map/reduce_scatter | solution.py:430
  762.2 190.1 %collective-permute-start.136 = (bf16[1,256,1408]{2,1,0:T(8,128)(2,1)}, bf16[1,256,1408]{2,1,0:T(8,128)(2,1)}, u32[]{:S(2)}, u32[]{:S(2)}) collective-permute-start(bf16[1,256,1408]{2,1,0:T(8,128)(2,1)} %reduce-scatter.9.cloned.1.call-done), channel_id=1, source_target_pairs={{0,16},{1,17},{2,18},{3,19},{4,20},{5,21},{6,22},{7,23},{8,24},{9,... | collective-permute-start | bytes 2162696 | tf_op jit(solution)/shard_map/ppermute | solution.py:776
  796.5 46.7 %collective-permute-start.92 = (bf16[1,1024,1408]{2,1,0:T(8,128)(2,1)}, bf16[1,1024,1408]{2,1,0:T(8,128)(2,1)}, u32[]{:S(2)}, u32[]{:S(2)}) collective-permute-start(bf16[1,1024,1408]{2,1,0:T(8,128)(2,1)} %fusion.11), channel_id=1, source_target_pairs={{0,16},{16,0},{1,17},{17,1},{2,18},{18,2},{3,19},{19,3},{4,20},{20... | collective-permute-start | bytes 8650760 | tf_op jit(solution)/shard_map/ppermute | solution.py:211
  807.2 186.1 %reduce-scatter.19.cloned.1.call-start = ((), (), s32[]{:S(2)}) async-start(), calls=%async_computation.18 | async-start | bytes 3604480 | tf_op jit(solution)/shard_map/reduce_scatter | solution.py:430
  856.9 308.1 %reduce-scatter.23.cloned.1.call-start = ((), (), s32[]{:S(2)}) async-start(), calls=%async_computation.20 | async-start | bytes 4915200 | tf_op jit(solution)/shard_map/reduce_scatter | solution.py:430
  947.5 44.0 %collective-permute-start.101 = (bf16[2,512,512]{2,1,0:T(8,128)(2,1)S(1)}, bf16[2,512,512]{2,1,0:T(8,128)(2,1)S(1)}, u32[]{:S(2)}, u32[]{:S(2)}) collective-permute-start(bf16[2,512,512]{2,1,0:T(8,128)(2,1)S(1)} %add_convert_fusion.2), channel_id=1, source_target_pairs={{4,0},{8,12},{5,1},{9,13},{6,2},{10,14},{7,3},{11,15},{20,16},{24,... | collective-permute-start | bytes 3145736 | tf_op jit(solution)/shard_map/ppermute | solution.py:268
  952.3 111.9 %collective-permute-start.137 = (bf16[1,256,1408]{2,1,0:T(8,128)(2,1)}, bf16[1,256,1408]{2,1,0:T(8,128)(2,1)}, u32[]{:S(2)}, u32[]{:S(2)}) collective-permute-start(bf16[1,256,1408]{2,1,0:T(8,128)(2,1)} %reduce-scatter.17.cloned.1.call-done), channel_id=1, source_target_pairs={{16,0},{17,1},{18,2},{19,3},{20,4},{21,5},{22,6},{23,7},{24,8},{25... | collective-permute-start | bytes 2162696 | tf_op jit(solution)/shard_map/ppermute | solution.py:775
  1008.8 180.9 %reduce-scatter.21.cloned.1.call-start = ((), (), s32[]{:S(2)}) async-start(), calls=%async_computation.19 | async-start | bytes 3932160 | tf_op jit(solution)/shard_map/reduce_scatter | solution.py:430
  1061.4 39.2 %collective-permute-start.121 = (bf16[128,2048]{1,0:T(8,128)(2,1)}, bf16[128,2048]{1,0:T(8,128)(2,1)S(1)}, u32[]{:S(2)}, u32[]{:S(2)}) collective-permute-start(bf16[128,2048]{1,0:T(8,128)(2,1)} %reshape.1040), channel_id=1, source_target_pairs={{12,0},{28,4},{8,8},{24,12},{13,1},{29,5},{9,9},{25,13},{14,2},{30... | collective-permute-start | bytes 1572872 | tf_op jit(solution)/shard_map/ppermute | solution.py:523
  1069.3 50.3 %collective-permute-start.116 = (bf16[2,256,1024]{2,1,0:T(8,128)(2,1)}, bf16[2,256,1024]{2,1,0:T(8,128)(2,1)}, u32[]{:S(2)}, u32[]{:S(2)}) collective-permute-start(bf16[2,256,1024]{2,1,0:T(8,128)(2,1)} %get-tuple-element.373), channel_id=1, source_target_pairs={{16,18},{17,19},{18,16},{19,17},{20,22},{21,23},{22,20},{23,21},{2... | collective-permute-start | bytes 3145736 | tf_op jit(solution)/shard_map/ppermute | solution.py:531
  1071.1 55.3 %collective-permute-start.118 = (bf16[2,256,1024]{2,1,0:T(8,128)(2,1)}, bf16[2,256,1024]{2,1,0:T(8,128)(2,1)}, u32[]{:S(2)}, u32[]{:S(2)}) collective-permute-start(bf16[2,256,1024]{2,1,0:T(8,128)(2,1)} %get-tuple-element.372), channel_id=1, source_target_pairs={{16,17},{17,16},{18,19},{19,18},{20,21},{21,20},{22,23},{23,22},{2... | collective-permute-start | bytes 3145736 | tf_op jit(solution)/shard_map/ppermute | solution.py:531
  1139.1 37.4 %collective-permute-start.132 = (bf16[1,256,512]{2,1,0:T(8,128)(2,1)S(1)}, bf16[1,256,512]{2,1,0:T(8,128)(2,1)}, u32[]{:S(2)}, u32[]{:S(2)}) collective-permute-start(bf16[1,256,512]{2,1,0:T(8,128)(2,1)S(1)} %copy-done.144), channel_id=1, source_target_pairs={{0,16},{1,17},{2,18},{3,19},{4,20},{5,21},{6,22},{7,23},{8,24},{9,... | collective-permute-start | bytes 786440 | tf_op jit(solution)/shard_map/ppermute | solution.py:776
  1152.5 42.9 %collective-permute-start.130 = (bf16[3,256,512]{2,1,0:T(8,128)(2,1)}, bf16[3,256,512]{2,1,0:T(8,128)(2,1)}, u32[]{:S(2)}, u32[]{:S(2)}) collective-permute-start(bf16[3,256,512]{2,1,0:T(8,128)(2,1)} %reduce-scatter.15.cloned.1.call-done), channel_id=1, source_target_pairs={{0,16},{1,17},{2,18},{3,19},{4,20},{5,21},{6,22},{7,23},{8,24},{9,... | collective-permute-start | bytes 2359304 | tf_op jit(solution)/shard_map/ppermute | solution.py:776
  (324 other events, 4375.2 us)
Sparse Core Ops, SparseCore 0:
  39.8 87.4 all-gather.5
  133.5 156.3 all-gather.9
  292.0 78.9 all-gather.7
  373.0 105.2 all-gather.13
  493.6 65.8 all-gather.11
  561.7 54.8 reduce-scatter.8
  619.7 55.8 reduce-scatter.10
  703.1 75.1 reduce-scatter.12
  781.2 60.5 reduce-scatter.14
  844.5 56.1 reduce-scatter.16
  903.6 63.6 reduce-scatter.18
  1008.9 94.2 reduce-scatter.22
  1115.8 58.9 reduce-scatter.20

commit v3 on v2

--- a/solution.py
+++ b/solution.py
@@ -709,6 +709,9 @@
         queries, key_values, attended, attended_low, log_total = kept_attention[layer]
         attended_grad = into(branch_grad, [half[0] for half in out_weights[layer]]).astype(BF16)
         if layer == 0:
+            out_total = weight_grad(branch_grad, [attended_low])
+            attended_grad, out_total = lax.optimization_barrier((attended_grad, out_total))
+            gate_total = jnp.concatenate([gate_total, out_total], axis=2)
             last = down_forward(
                 hidden_one, after(kept_feed_one[2], attended_grad), down_weights[1]
             )
@@ -719,16 +722,17 @@
         gate_weight_grad = scatter_weight_grad(gate_total)
         key_value_grad = after(scatter_chunks(key_value_grads), gate_weight_grad)
         if layer == 0:
-            home_one = send_home(1, after(jnp.concatenate([last, input_grads[1]]), query_grad))
-            key_value_grad, home_one = lax.optimization_barrier((key_value_grad, home_one))
-        out_total = weight_grad(branch_grad, [attended_low])
+            home_one = send_home(
+                1, after(jnp.concatenate([last, input_grads[1]]), key_value_grad)
+            )
+        if layer == 1:
+            out_total = weight_grad(branch_grad, [attended_low])
+            up_total = jnp.concatenate([up_total, out_total], axis=2)
         query_grad = rotate(query_grad, tables, -1.0).astype(BF16)
-        key_value_grad, out_total, query_grad = lax.optimization_barrier(
-            (key_value_grad, out_total, query_grad)
+        key_value_grad, up_total, query_grad = lax.optimization_barrier(
+            (key_value_grad, up_total, query_grad)
         )
-        up_weight_grad = scatter_weight_grad(
-            after(jnp.concatenate([up_total, out_total], axis=2), key_value_grad)
-        )
+        up_weight_grad = scatter_weight_grad(up_total)
         key_grad = rotate(key_value_grad[0], tables, -1.0).astype(BF16)
         projected = (query_grad, key_grad, key_value_grad[1].astype(BF16))
         partial = projected_partial(projected, qkv_weights[layer])
@@ -747,9 +751,11 @@
             grad_full = after(tp_gather(grad), up_weight_grad)
         norm_grads = unsplit(jnp.stack([gain_first, gain_second, shift_first, shift_second]))
         small_grads[layer] = (norm_grads, bias_grad)
-        feed_width = gate_weight_grad.shape[2]
-        gate_up_grad = jnp.concatenate([gate_weight_grad, up_weight_grad[:, :, :feed_width]])
-        out_grad = up_weight_grad[:, :, feed_width:]
+        feed_width = down_grad.shape[2]
+        gate_up_grad = jnp.concatenate(
+            [gate_weight_grad[:, :, :feed_width], up_weight_grad[:, :, :feed_width]]
+        )
+        out_grad = (up_weight_grad if layer == 1 else gate_weight_grad)[:, :, feed_width:]
         scattered[layer] = (attention_grad, out_grad, gate_up_grad, down_grad)
 
     norm_grads, bias_grads = [jnp.stack(parts) for parts in zip(*small_grads)]
@@ -763,7 +769,7 @@
     norm_grads = packed[:norm_rows].reshape(norm_grads.shape)
     bias_grads = packed[norm_rows:].reshape(bias_grads.shape)
     norm_grads, bias_grads = by_core(norm_grads[0], norm_grads[1]), by_core(bias_grads[0], bias_grads[1])
-    home_grad = spread_home(0, home_grad)
+    home_grad = list(after(spread_home(0, home_grad), attention_grad))
     layer_outputs = assemble(
         [by_core(zero, one[:, :piece_rows]) for zero, one in zip(home_zero, home_one)], BF16
     )

time: 1220 us -> 1220 us (level)
    ppermute x4, waiting for transfers between devices: 77.4 us -> 105 us  [across(): return [lax.ppermute(block, 'ctx', pairs) for block in blocks]]
    ppermute x78, waiting for transfers between devices: 217 us -> 202 us  [exchange(): lax.ppermute(block, axis, [(i, i ^ bit) for i in range(lax.axis_size(axis...]
    ppermute x6, waiting for transfers between devices: 32 us -> 18.7 us  [send_home(): lax.ppermute(piece, both, [(seat(i, half), layer * count + i) for i in ra...]
    unnamed x412 -> x442, local copies, waits for them, and re-layouts: 27.6 us -> 28.6 us
  transfers between devices with their start and end apart: 151 -> 151, of which waited for: 78 -> 74; matrix products, arithmetic and copies ran while one was open for 37% -> 37% of each run, Pallas kernels for 4% -> 4%
where the time goes in v3:
time: 1220 us; the launch traced here: 1200 us
  waiting for transfers between devices  473 us (39%)
  matrix products  220 us (18%)
  starting transfers between devices  190 us (16%)
  other arithmetic  149 us (12%)
  local copies, waits for them, and re-layouts  106 us (9%)
  Pallas kernels  44.6 us (4%)
  between operations  19.2 us (2%)
    ppermute x78, waiting for transfers between devices, exchange(): lax.ppermute(block, axis, [(i, i ^ bit) for i in range(lax.axis_size(axis...  202 us
    ppermute x4, waiting for transfers between devices, across(): return [lax.ppermute(block, 'ctx', pairs) for block in blocks]  105 us
    ppermute x78, starting transfers between devices, exchange(): lax.ppermute(block, axis, [(i, i ^ bit) for i in range(lax.axis_size(axis...  102 us
    all_gather x5, waiting for transfers between devices, gather(): return lax.all_gather(after(piece, *others), 'ctx', axis=1, tiled=True)  97.2 us
    dot_general x36, matrix products, dot(): return jnp.dot(left, right, preferred_element_type=F32)  92.6 us
    dot_general x28, matrix products, token_sum(): lax.dot_general(left, right, CONTRACT_FIRST, preferred_element_type=F32)  64.7 us
    dot_general x28, matrix products, dot_back(): lax.dot_general(left, right, CONTRACT_LAST, preferred_element_type=F32)  62.6 us
    unnamed x442, local copies, waits for them, and re-layouts  28.6 us
  transfers between devices with their start and end apart: 151, of which 74 were waited for; matrix products, arithmetic and copies ran while one was open for 37% of the time, Pallas kernels for 4%

profile of v3, /device:TPU:0, one launch (start us, length us, event | category | flops | bytes accessed | tf_op | source)
XLA Modules:
  0.0 1201.4 jit_solution(10743400210519675561)
XLA Ops:
  81.5 6.8 collective-permute-done.9
  92.6 10.0 collective-permute-done.10
  102.6 24.6 %all-gather.6.cloned.1.call-done = bf16[4,1024,512]{2,1,0:T(8,128)(2,1)} async-done(((bf16[4,256,512]{2,1,0:T(8,128)(2,1)}), bf16[4,1024,512]{2,1,0:T(8,128)(2,1)}) %all-gather.6.cloned.1.call-update) | async-done | bytes 4194320 | tf_op jit(solution)/shard_map/all_gather | solution.py:601
  192.0 9.6 attend.2
  207.1 6.4 collective-permute-done.20
  238.4 12.9 %collective-permute-done.24 = bf16[128,1024]{1,0:T(8,128)(2,1)S(1)} collective-permute-done((bf16[128,1024]{1,0:T(8,128)(2,1)S(1)}, bf16[128,1024]{1,0:T(8,128)(2,1)S(1)}, u32[]{:S(2)}, u32[]{:S(2)}) %collective-permute-start.24) | collective-permute-done | bytes 262176 | tf_op jit(solution)/shard_map/ppermute | solution.py:215
  255.1 7.4 collective-permute-done.27
  265.9 23.8 %all-gather.10.cloned.1.call-done = bf16[3,1024,1408]{2,1,0:T(8,128)(2,1)} async-done(((bf16[3,256,1408]{2,1,0:T(8,128)(2,1)}), bf16[3,1024,1408]{2,1,0:T(8,128)(2,1)}) %all-gather.10.cloned.1.call-update) | async-done | bytes 8650768 | tf_op jit(solution)/shard_map/all_gather | solution.py:601
  324.6 7.3 collective-permute-done.33
  356.7 7.3 collective-permute-done.40
  399.4 9.8 collective-permute-done.45
  421.9 9.6 attend.3
  436.7 6.7 collective-permute-done.49
  455.1 23.0 %all-gather.14.cloned.1.call-done = bf16[2,1024,1408]{2,1,0:T(8,128)(2,1)} async-done(((bf16[2,256,1408]{2,1,0:T(8,128)(2,1)}), bf16[2,1024,1408]{2,1,0:T(8,128)(2,1)}) %all-gather.14.cloned.1.call-update) | async-done | bytes 5767184 | tf_op jit(solution)/shard_map/all_gather | solution.py:601
  518.8 6.4 multiply_convert_fusion.4
  542.7 20.1 %all-gather.12.cloned.1.call-done = bf16[1,1024,1408]{2,1,0:T(8,128)(2,1)} async-done(((bf16[1,256,1408]{2,1,0:T(8,128)(2,1)}), bf16[1,1024,1408]{2,1,0:T(8,128)(2,1)}) %all-gather.12.cloned.1.call-update) | async-done | bytes 2883600 | tf_op jit(solution)/shard_map/all_gather | solution.py:601
  643.3 12.7 %attend_back.2 = (f32[512,512]{1,0:T(8,128)S(1)}, bf16[2,512,512]{2,1,0:T(8,128)(2,1)S(1)}, bf16[2,512,512]{2,1,0:T(8,128)(2,1)}, bf16[2,512,512]{2,1,0:T(8,128)(2,1)S(1)}, bf16[2,512,512]{2,1,0:T(8,128)(2,1)}) custom-call(s32[4]{0:T(128)S(1)} %add_convert_fusion.12.refs_0_, bf16[512,512]{1,0:T(8,128)(2,1)S(1)} %copy-done.7, ...), custom_call_target="tpu_custom_call" | custom-call | flops 10737418240 | bytes 12582912 | tf_op jit(solution)/shard_map/attend_back/pallas_call | solution.py:181
  670.4 29.6 %collective-permute-done.77 = bf16[2,512,512]{2,1,0:T(8,128)(2,1)} collective-permute-done((bf16[2,512,512]{2,1,0:T(8,128)(2,1)}, bf16[2,512,512]{2,1,0:T(8,128)(2,1)}, u32[]{:S(2)}, u32[]{:S(2)}) %collective-permute-start.77) | collective-permute-done | bytes 1048608 | tf_op jit(solution)/shard_map/ppermute | solution.py:268
  736.7 7.1 collective-permute-done.81
  775.6 7.5 reduce-scatter.13.cloned.1.call-done
  900.8 12.8 %attend_back.3 = (f32[512,512]{1,0:T(8,128)S(1)}, bf16[2,512,512]{2,1,0:T(8,128)(2,1)S(1)}, bf16[2,512,512]{2,1,0:T(8,128)(2,1)S(1)}, bf16[2,512,512]{2,1,0:T(8,128)(2,1)S(1)}, bf16[2,512,512]{2,1,0:T(8,128)(2,1)}) custom-call(s32[4]{0:T(128)S(1)} %add_convert_fusion.12.refs_0_, bf16[512,512]{1,0:T(8,128)(2,1)S(1)} %copy-done.5, ...), custom_call_target="tpu_custom_call" | custom-call | flops 10737418240 | bytes 12582912 | tf_op jit(solution)/shard_map/attend_back/pallas_call | solution.py:181
  937.7 63.9 %collective-permute-done.106 = bf16[2,512,512]{2,1,0:T(8,128)(2,1)} collective-permute-done((bf16[2,512,512]{2,1,0:T(8,128)(2,1)}, bf16[2,512,512]{2,1,0:T(8,128)(2,1)}, u32[]{:S(2)}, u32[]{:S(2)}) %collective-permute-start.106) | collective-permute-done | bytes 1048608 | tf_op jit(solution)/shard_map/ppermute | solution.py:268
  1097.5 13.0 %collective-permute-done.121 = bf16[128,2048]{1,0:T(8,128)(2,1)} collective-permute-done((bf16[128,2048]{1,0:T(8,128)(2,1)}, bf16[128,2048]{1,0:T(8,128)(2,1)}, u32[]{:S(2)}, u32[]{:S(2)}) %collective-permute-start.121) | collective-permute-done | bytes 524320 | tf_op jit(solution)/shard_map/ppermute | solution.py:523
  1141.7 12.1 %collective-permute-done.123 = bf16[2,2,128,1024]{3,2,1,0:T(8,128)(2,1)S(1)} collective-permute-done((bf16[2,2,128,1024]{3,2,1,0:T(8,128)(2,1)S(1)}, bf16[2,2,128,1024]{3,2,1,0:T(8,128)(2,1)S(1)}, u32[]{:S(2)}, u32[]{:S(2)}) %collective-permute-start.123) | collective-permute-done | bytes 1048608 | tf_op jit(solution)/shard_map/ppermute | solution.py:531
  (1210 shorter events, 831.9 us)
Async XLA Ops:
  7.2 120.0 %all-gather.6.cloned.1.call-start = ((), (), s32[]{:S(2)}) async-start(), calls=%async_computation.8 | async-start | bytes 5242880 | tf_op jit(solution)/shard_map/all_gather | solution.py:601
  39.5 250.2 %all-gather.10.cloned.1.call-start = ((), (), s32[]{:S(2)}) async-start(), calls=%async_computation.10 | async-start | bytes 10813440 | tf_op jit(solution)/shard_map/all_gather | solution.py:601
  133.2 237.6 %all-gather.8.cloned.1.call-start = ((), (), s32[]{:S(2)}) async-start(), calls=%async_computation.9 | async-start | bytes 5242880 | tf_op jit(solution)/shard_map/all_gather | solution.py:601
  290.1 188.0 %all-gather.14.cloned.1.call-start = ((), (), s32[]{:S(2)}) async-start(), calls=%async_computation.12 | async-start | bytes 7208960 | tf_op jit(solution)/shard_map/all_gather | solution.py:601
  370.9 191.9 %all-gather.12.cloned.1.call-start = ((), (), s32[]{:S(2)}) async-start(), calls=%async_computation.11 | async-start | bytes 3604480 | tf_op jit(solution)/shard_map/all_gather | solution.py:601
  478.1 37.1 %collective-permute-start.59 = (bf16[2,1024,1408]{2,1,0:T(8,128)(2,1)}, bf16[2,1024,1408]{2,1,0:T(8,128)(2,1)}, u32[]{:S(2)}, u32[]{:S(2)}) collective-permute-start(bf16[2,1024,1408]{2,1,0:T(8,128)(2,1)} %all-gather.14.cloned.1.call-done), channel_id=1, source_target_pairs={{0,16},{16,0},{1,17},{17,1},{2,18},{18,2},{3,19},{19,3},{4,20},{20... | collective-permute-start | bytes 17301512 | tf_op jit(solution)/shard_map/ppermute | solution.py:211
  496.3 159.7 %reduce-scatter.9.cloned.1.call-start = ((), (), s32[]{:S(2)}) async-start(), calls=%async_computation.13 | async-start | bytes 3604480 | tf_op jit(solution)/shard_map/reduce_scatter | solution.py:430
  562.9 140.4 %reduce-scatter.11.cloned.1.call-start = ((), (), s32[]{:S(2)}) async-start(), calls=%async_computation.14 | async-start | bytes 3604480 | tf_op jit(solution)/shard_map/reduce_scatter | solution.py:430
  622.4 160.7 %reduce-scatter.13.cloned.1.call-start = ((), (), s32[]{:S(2)}) async-start(), calls=%async_computation.15 | async-start | bytes 4915200 | tf_op jit(solution)/shard_map/reduce_scatter | solution.py:430
  663.5 36.5 %collective-permute-start.77 = (bf16[2,512,512]{2,1,0:T(8,128)(2,1)}, bf16[2,512,512]{2,1,0:T(8,128)(2,1)}, u32[]{:S(2)}, u32[]{:S(2)}) collective-permute-start(bf16[2,512,512]{2,1,0:T(8,128)(2,1)} %add_convert_fusion.7), channel_id=1, source_target_pairs={{4,0},{8,12},{5,1},{9,13},{6,2},{10,14},{7,3},{11,15},{20,16},{24,... | collective-permute-start | bytes 3145736 | tf_op jit(solution)/shard_map/ppermute | solution.py:268
  709.0 157.5 %reduce-scatter.15.cloned.1.call-start = ((), (), s32[]{:S(2)}) async-start(), calls=%async_computation.16 | async-start | bytes 3932160 | tf_op jit(solution)/shard_map/reduce_scatter | solution.py:430
  767.3 154.9 %reduce-scatter.17.cloned.1.call-start = ((), (), s32[]{:S(2)}) async-start(), calls=%async_computation.17 | async-start | bytes 3604480 | tf_op jit(solution)/shard_map/reduce_scatter | solution.py:430
  786.7 45.4 %collective-permute-start.103 = (bf16[1,1024,1408]{2,1,0:T(8,128)(2,1)S(1)}, bf16[1,1024,1408]{2,1,0:T(8,128)(2,1)S(1)}, u32[]{:S(2)}, u32[]{:S(2)}) collective-permute-start(bf16[1,1024,1408]{2,1,0:T(8,128)(2,1)S(1)} %fusion.13), channel_id=1, source_target_pairs={{0,16},{16,0},{1,17},{17,1},{2,18},{18,2},{3,19},{19,3},{4,20},{20... | collective-permute-start | bytes 8650760 | tf_op jit(solution)/shard_map/ppermute | solution.py:211
  799.0 38.1 %collective-permute-start.92 = (bf16[1,1024,1408]{2,1,0:T(8,128)(2,1)}, bf16[1,1024,1408]{2,1,0:T(8,128)(2,1)}, u32[]{:S(2)}, u32[]{:S(2)}) collective-permute-start(bf16[1,1024,1408]{2,1,0:T(8,128)(2,1)} %fusion.11), channel_id=1, source_target_pairs={{0,16},{16,0},{1,17},{17,1},{2,18},{18,2},{3,19},{19,3},{4,20},{20... | collective-permute-start | bytes 8650760 | tf_op jit(solution)/shard_map/ppermute | solution.py:211
  835.7 169.2 %reduce-scatter.19.cloned.1.call-start = ((), (), s32[]{:S(2)}) async-start(), calls=%async_computation.18 | async-start | bytes 4915200 | tf_op jit(solution)/shard_map/reduce_scatter | solution.py:430
  868.2 56.7 %collective-permute-start.136 = (bf16[1,256,1408]{2,1,0:T(8,128)(2,1)}, bf16[1,256,1408]{2,1,0:T(8,128)(2,1)}, u32[]{:S(2)}, u32[]{:S(2)}) collective-permute-start(bf16[1,256,1408]{2,1,0:T(8,128)(2,1)} %reduce-scatter.9.cloned.1.call-done), channel_id=1, source_target_pairs={{0,16},{1,17},{2,18},{3,19},{4,20},{5,21},{6,22},{7,23},{8,24},{9,... | collective-permute-start | bytes 2162696 | tf_op jit(solution)/shard_map/ppermute | solution.py:782
  880.7 276.4 %reduce-scatter.23.cloned.1.call-start = ((), (), s32[]{:S(2)}) async-start(), calls=%async_computation.20 | async-start | bytes 3604480 | tf_op jit(solution)/shard_map/reduce_scatter | solution.py:430
  889.1 268.0 %collective-permute-start.134 = (bf16[2,256,1408]{2,1,0:T(8,128)(2,1)}, bf16[2,256,1408]{2,1,0:T(8,128)(2,1)}, u32[]{:S(2)}, u32[]{:S(2)}) collective-permute-start(bf16[2,256,1408]{2,1,0:T(8,128)(2,1)} %pad_maximum_fusion.9), channel_id=1, source_target_pairs={{0,16},{1,17},{2,18},{3,19},{4,20},{5,21},{6,22},{7,23},{8,24},{9,... | collective-permute-start | bytes 4325384 | tf_op jit(solution)/shard_map/ppermute | solution.py:782
  892.3 128.2 %collective-permute-start.132 = (bf16[1,256,512]{2,1,0:T(8,128)(2,1)}, bf16[1,256,512]{2,1,0:T(8,128)(2,1)}, u32[]{:S(2)}, u32[]{:S(2)}) collective-permute-start(bf16[1,256,512]{2,1,0:T(8,128)(2,1)} %slice.1436), channel_id=1, source_target_pairs={{0,16},{1,17},{2,18},{3,19},{4,20},{5,21},{6,22},{7,23},{8,24},{9,... | collective-permute-start | bytes 786440 | tf_op jit(solution)/shard_map/ppermute | solution.py:782
  929.8 71.8 %collective-permute-start.106 = (bf16[2,512,512]{2,1,0:T(8,128)(2,1)}, bf16[2,512,512]{2,1,0:T(8,128)(2,1)}, u32[]{:S(2)}, u32[]{:S(2)}) collective-permute-start(bf16[2,512,512]{2,1,0:T(8,128)(2,1)} %add_convert_fusion.2), channel_id=1, source_target_pairs={{4,0},{8,12},{5,1},{9,13},{6,2},{10,14},{7,3},{11,15},{20,16},{24,... | collective-permute-start | bytes 3145736 | tf_op jit(solution)/shard_map/ppermute | solution.py:268
  1013.3 162.1 %reduce-scatter.21.cloned.1.call-start = ((), (), s32[]{:S(2)}) async-start(), calls=%async_computation.19 | async-start | bytes 3932160 | tf_op jit(solution)/shard_map/reduce_scatter | solution.py:430
  1026.2 49.4 %collective-permute-start.113 = (bf16[3,1024,512]{2,1,0:T(8,128)(2,1)}, bf16[3,1024,512]{2,1,0:T(8,128)(2,1)}, u32[]{:S(2)}, u32[]{:S(2)}) collective-permute-start(bf16[3,1024,512]{2,1,0:T(8,128)(2,1)} %pad_maximum_fusion.3), channel_id=1, source_target_pairs={{0,16},{16,0},{1,17},{17,1},{2,18},{18,2},{3,19},{19,3},{4,20},{20... | collective-permute-start | bytes 9437192 | tf_op jit(solution)/shard_map/ppermute | solution.py:211
  1096.7 39.2 %collective-permute-start.118 = (bf16[2,256,1024]{2,1,0:T(8,128)(2,1)S(1)}, bf16[2,256,1024]{2,1,0:T(8,128)(2,1)S(1)}, u32[]{:S(2)}, u32[]{:S(2)}) collective-permute-start(bf16[2,256,1024]{2,1,0:T(8,128)(2,1)S(1)} %get-tuple-element.376), channel_id=1, source_target_pairs={{16,17},{17,16},{18,19},{19,18},{20,21},{21,20},{22,23},{23,22},{2... | collective-permute-start | bytes 3145736 | tf_op jit(solution)/shard_map/ppermute | solution.py:531
  1135.9 53.2 %collective-permute-start.130 = (bf16[3,256,512]{2,1,0:T(8,128)(2,1)}, bf16[3,256,512]{2,1,0:T(8,128)(2,1)}, u32[]{:S(2)}, u32[]{:S(2)}) collective-permute-start(bf16[3,256,512]{2,1,0:T(8,128)(2,1)} %reduce-scatter.15.cloned.1.call-done), channel_id=1, source_target_pairs={{0,16},{1,17},{2,18},{3,19},{4,20},{5,21},{6,22},{7,23},{8,24},{9,... | collective-permute-start | bytes 2359304 | tf_op jit(solution)/shard_map/ppermute | solution.py:782
  (339 other events, 4456.1 us)
Sparse Core Ops, SparseCore 0:
  39.7 87.4 all-gather.5
  133.3 156.3 all-gather.9
  291.9 78.9 all-gather.7
  372.8 105.2 all-gather.13
  496.4 66.2 all-gather.11
  564.9 54.8 reduce-scatter.8
  622.5 55.6 reduce-scatter.10
  709.1 74.0 reduce-scatter.12
  786.0 60.6 reduce-scatter.14
  848.8 56.1 reduce-scatter.16
  907.9 88.6 reduce-scatter.18
  1013.4 58.1 reduce-scatter.22
  1093.6 64.3 reduce-scatter.20

commit v4 on v3

--- a/solution.py
+++ b/solution.py
@@ -769,7 +769,7 @@
     norm_grads = packed[:norm_rows].reshape(norm_grads.shape)
     bias_grads = packed[norm_rows:].reshape(bias_grads.shape)
     norm_grads, bias_grads = by_core(norm_grads[0], norm_grads[1]), by_core(bias_grads[0], bias_grads[1])
-    home_grad = list(after(spread_home(0, home_grad), attention_grad))
+    home_grad, home_one = after((spread_home(0, home_grad), home_one), attention_grad)
     layer_outputs = assemble(
         [by_core(zero, one[:, :piece_rows]) for zero, one in zip(home_zero, home_one)], BF16
     )

time: 1220 us -> 1240 us (1.016)
    ppermute x11, waiting for transfers between devices: 18.2 us -> 5.55 us  [send(): return lax.ppermute(block, ('section', 'tp'), pairs)]
  transfers between devices with their start and end apart: 151 -> 151, of which waited for: 74 -> 77; matrix products, arithmetic and copies ran while one was open for 37% -> 37% of each run, Pallas kernels for 4% -> 4%
where the time goes in v4:
time: 1240 us; the launch traced here: 1220 us
  waiting for transfers between devices  475 us (38%)
  matrix products  223 us (18%)
  starting transfers between devices  197 us (16%)
  other arithmetic  154 us (12%)
  local copies, waits for them, and re-layouts  107 us (9%)
  Pallas kernels  44.2 us (4%)
  between operations  18.9 us (2%)
    ppermute x78, waiting for transfers between devices, exchange(): lax.ppermute(block, axis, [(i, i ^ bit) for i in range(lax.axis_size(axis...  210 us
    ppermute x78, starting transfers between devices, exchange(): lax.ppermute(block, axis, [(i, i ^ bit) for i in range(lax.axis_size(axis...  110 us
    ppermute x4, waiting for transfers between devices, across(): return [lax.ppermute(block, 'ctx', pairs) for block in blocks]  104 us
    all_gather x5, waiting for transfers between devices, gather(): return lax.all_gather(after(piece, *others), 'ctx', axis=1, tiled=True)  96.1 us
    dot_general x36, matrix products, dot(): return jnp.dot(left, right, preferred_element_type=F32)  93 us
    dot_general x28, matrix products, token_sum(): lax.dot_general(left, right, CONTRACT_FIRST, preferred_element_type=F32)  66.7 us
    dot_general x28, matrix products, dot_back(): lax.dot_general(left, right, CONTRACT_LAST, preferred_element_type=F32)  63.7 us
    unnamed x442, local copies, waits for them, and re-layouts  31.9 us
  transfers between devices with their start and end apart: 151, of which 77 were waited for; matrix products, arithmetic and copies ran while one was open for 37% of the time, Pallas kernels for 4%

profile of v4, /device:TPU:0, one launch (start us, length us, event | category | flops | bytes accessed | tf_op | source)
XLA Modules:
  0.0 1219.2 jit_solution(11221582975411002878)
XLA Ops:
  83.5 5.8 collective-permute-done.9
  93.6 9.9 collective-permute-done.10
  103.6 23.7 %all-gather.6.cloned.1.call-done = bf16[4,1024,512]{2,1,0:T(8,128)(2,1)} async-done(((bf16[4,256,512]{2,1,0:T(8,128)(2,1)}), bf16[4,1024,512]{2,1,0:T(8,128)(2,1)}) %all-gather.6.cloned.1.call-update) | async-done | bytes 4194320 | tf_op jit(solution)/shard_map/all_gather | solution.py:601
  192.0 9.4 attend.2
  206.9 6.4 collective-permute-done.20
  238.1 14.7 %collective-permute-done.24 = bf16[128,1024]{1,0:T(8,128)(2,1)S(1)} collective-permute-done((bf16[128,1024]{1,0:T(8,128)(2,1)S(1)}, bf16[128,1024]{1,0:T(8,128)(2,1)S(1)}, u32[]{:S(2)}, u32[]{:S(2)}) %collective-permute-start.24) | collective-permute-done | bytes 262176 | tf_op jit(solution)/shard_map/ppermute | solution.py:215
  256.5 7.5 collective-permute-done.27
  267.4 22.4 %all-gather.10.cloned.1.call-done = bf16[3,1024,1408]{2,1,0:T(8,128)(2,1)} async-done(((bf16[3,256,1408]{2,1,0:T(8,128)(2,1)}), bf16[3,1024,1408]{2,1,0:T(8,128)(2,1)}) %all-gather.10.cloned.1.call-update) | async-done | bytes 8650768 | tf_op jit(solution)/shard_map/all_gather | solution.py:601
  307.3 6.5 multiply_convert_fusion.5
  324.9 7.3 collective-permute-done.33
  356.9 7.3 collective-permute-done.40
  399.0 9.8 collective-permute-done.45
  421.5 9.4 attend.3
  436.0 6.8 collective-permute-done.49
  453.7 24.5 %all-gather.14.cloned.1.call-done = bf16[2,1024,1408]{2,1,0:T(8,128)(2,1)} async-done(((bf16[2,256,1408]{2,1,0:T(8,128)(2,1)}), bf16[2,1024,1408]{2,1,0:T(8,128)(2,1)}) %all-gather.14.cloned.1.call-update) | async-done | bytes 5767184 | tf_op jit(solution)/shard_map/all_gather | solution.py:601
  517.3 6.5 multiply_convert_fusion.4
  539.4 20.0 %all-gather.12.cloned.1.call-done = bf16[1,1024,1408]{2,1,0:T(8,128)(2,1)} async-done(((bf16[1,256,1408]{2,1,0:T(8,128)(2,1)}), bf16[1,1024,1408]{2,1,0:T(8,128)(2,1)}) %all-gather.12.cloned.1.call-update) | async-done | bytes 2883600 | tf_op jit(solution)/shard_map/all_gather | solution.py:601
  640.3 12.7 %attend_back.2 = (f32[512,512]{1,0:T(8,128)S(1)}, bf16[2,512,512]{2,1,0:T(8,128)(2,1)S(1)}, bf16[2,512,512]{2,1,0:T(8,128)(2,1)}, bf16[2,512,512]{2,1,0:T(8,128)(2,1)S(1)}, bf16[2,512,512]{2,1,0:T(8,128)(2,1)}) custom-call(s32[4]{0:T(128)S(1)} %add_convert_fusion.12.refs_0_, bf16[512,512]{1,0:T(8,128)(2,1)S(1)} %copy-done.7, ...), custom_call_target="tpu_custom_call" | custom-call | flops 10737418240 | bytes 12582912 | tf_op jit(solution)/shard_map/attend_back/pallas_call | solution.py:181
  667.5 30.2 %collective-permute-done.77 = bf16[2,512,512]{2,1,0:T(8,128)(2,1)} collective-permute-done((bf16[2,512,512]{2,1,0:T(8,128)(2,1)}, bf16[2,512,512]{2,1,0:T(8,128)(2,1)}, u32[]{:S(2)}, u32[]{:S(2)}) %collective-permute-start.77) | collective-permute-done | bytes 1048608 | tf_op jit(solution)/shard_map/ppermute | solution.py:268
  735.2 7.2 collective-permute-done.81
  774.2 7.7 reduce-scatter.13.cloned.1.call-done
  900.2 12.8 %attend_back.3 = (f32[512,512]{1,0:T(8,128)S(1)}, bf16[2,512,512]{2,1,0:T(8,128)(2,1)S(1)}, bf16[2,512,512]{2,1,0:T(8,128)(2,1)S(1)}, bf16[2,512,512]{2,1,0:T(8,128)(2,1)S(1)}, bf16[2,512,512]{2,1,0:T(8,128)(2,1)}) custom-call(s32[4]{0:T(128)S(1)} %add_convert_fusion.12.refs_0_, bf16[512,512]{1,0:T(8,128)(2,1)S(1)} %copy-done.5, ...), custom_call_target="tpu_custom_call" | custom-call | flops 10737418240 | bytes 12582912 | tf_op jit(solution)/shard_map/attend_back/pallas_call | solution.py:181
  937.4 63.0 %collective-permute-done.102 = bf16[2,512,512]{2,1,0:T(8,128)(2,1)} collective-permute-done((bf16[2,512,512]{2,1,0:T(8,128)(2,1)}, bf16[2,512,512]{2,1,0:T(8,128)(2,1)}, u32[]{:S(2)}, u32[]{:S(2)}) %collective-permute-start.102) | collective-permute-done | bytes 1048608 | tf_op jit(solution)/shard_map/ppermute | solution.py:268
  1093.8 20.4 %collective-permute-done.109 = bf16[128,2048]{1,0:T(8,128)(2,1)S(1)} collective-permute-done((bf16[128,2048]{1,0:T(8,128)(2,1)}, bf16[128,2048]{1,0:T(8,128)(2,1)S(1)}, u32[]{:S(2)}, u32[]{:S(2)}) %collective-permute-start.109) | collective-permute-done | bytes 524320 | tf_op jit(solution)/shard_map/ppermute | solution.py:523
  (1213 shorter events, 848.5 us)
Async XLA Ops:
  7.2 120.1 %all-gather.6.cloned.1.call-start = ((), (), s32[]{:S(2)}) async-start(), calls=%async_computation.8 | async-start | bytes 5242880 | tf_op jit(solution)/shard_map/all_gather | solution.py:601
  39.6 250.2 %all-gather.10.cloned.1.call-start = ((), (), s32[]{:S(2)}) async-start(), calls=%async_computation.10 | async-start | bytes 10813440 | tf_op jit(solution)/shard_map/all_gather | solution.py:601
  133.2 237.7 %all-gather.8.cloned.1.call-start = ((), (), s32[]{:S(2)}) async-start(), calls=%async_computation.9 | async-start | bytes 5242880 | tf_op jit(solution)/shard_map/all_gather | solution.py:601
  290.2 188.0 %all-gather.14.cloned.1.call-start = ((), (), s32[]{:S(2)}) async-start(), calls=%async_computation.12 | async-start | bytes 7208960 | tf_op jit(solution)/shard_map/all_gather | solution.py:601
  370.9 188.5 %all-gather.12.cloned.1.call-start = ((), (), s32[]{:S(2)}) async-start(), calls=%async_computation.11 | async-start | bytes 3604480 | tf_op jit(solution)/shard_map/all_gather | solution.py:601
  493.3 159.6 %reduce-scatter.9.cloned.1.call-start = ((), (), s32[]{:S(2)}) async-start(), calls=%async_computation.13 | async-start | bytes 3604480 | tf_op jit(solution)/shard_map/reduce_scatter | solution.py:430
  559.5 141.4 %reduce-scatter.11.cloned.1.call-start = ((), (), s32[]{:S(2)}) async-start(), calls=%async_computation.14 | async-start | bytes 3604480 | tf_op jit(solution)/shard_map/reduce_scatter | solution.py:430
  619.5 162.5 %reduce-scatter.13.cloned.1.call-start = ((), (), s32[]{:S(2)}) async-start(), calls=%async_computation.15 | async-start | bytes 4915200 | tf_op jit(solution)/shard_map/reduce_scatter | solution.py:430
  660.5 37.1 %collective-permute-start.77 = (bf16[2,512,512]{2,1,0:T(8,128)(2,1)}, bf16[2,512,512]{2,1,0:T(8,128)(2,1)}, u32[]{:S(2)}, u32[]{:S(2)}) collective-permute-start(bf16[2,512,512]{2,1,0:T(8,128)(2,1)} %add_convert_fusion.7), channel_id=1, source_target_pairs={{4,0},{8,12},{5,1},{9,13},{6,2},{10,14},{7,3},{11,15},{20,16},{24,... | collective-permute-start | bytes 3145736 | tf_op jit(solution)/shard_map/ppermute | solution.py:268
  706.6 158.4 %reduce-scatter.15.cloned.1.call-start = ((), (), s32[]{:S(2)}) async-start(), calls=%async_computation.16 | async-start | bytes 3932160 | tf_op jit(solution)/shard_map/reduce_scatter | solution.py:430
  766.1 155.8 %reduce-scatter.17.cloned.1.call-start = ((), (), s32[]{:S(2)}) async-start(), calls=%async_computation.17 | async-start | bytes 3604480 | tf_op jit(solution)/shard_map/reduce_scatter | solution.py:430
  785.5 45.2 %collective-permute-start.99 = (bf16[1,1024,1408]{2,1,0:T(8,128)(2,1)S(1)}, bf16[1,1024,1408]{2,1,0:T(8,128)(2,1)S(1)}, u32[]{:S(2)}, u32[]{:S(2)}) collective-permute-start(bf16[1,1024,1408]{2,1,0:T(8,128)(2,1)S(1)} %fusion.13), channel_id=1, source_target_pairs={{0,16},{16,0},{1,17},{17,1},{2,18},{18,2},{3,19},{19,3},{4,20},{20... | collective-permute-start | bytes 8650760 | tf_op jit(solution)/shard_map/ppermute | solution.py:211
  797.6 38.0 %collective-permute-start.92 = (bf16[1,1024,1408]{2,1,0:T(8,128)(2,1)}, bf16[1,1024,1408]{2,1,0:T(8,128)(2,1)}, u32[]{:S(2)}, u32[]{:S(2)}) collective-permute-start(bf16[1,1024,1408]{2,1,0:T(8,128)(2,1)} %fusion.11), channel_id=1, source_target_pairs={{0,16},{16,0},{1,17},{17,1},{2,18},{18,2},{3,19},{19,3},{4,20},{20... | collective-permute-start | bytes 8650760 | tf_op jit(solution)/shard_map/ppermute | solution.py:211
  834.2 169.5 %reduce-scatter.19.cloned.1.call-start = ((), (), s32[]{:S(2)}) async-start(), calls=%async_computation.18 | async-start | bytes 4915200 | tf_op jit(solution)/shard_map/reduce_scatter | solution.py:430
  866.8 58.9 %collective-permute-start.136 = (bf16[1,256,1408]{2,1,0:T(8,128)(2,1)}, bf16[1,256,1408]{2,1,0:T(8,128)(2,1)}, u32[]{:S(2)}, u32[]{:S(2)}) collective-permute-start(bf16[1,256,1408]{2,1,0:T(8,128)(2,1)} %reduce-scatter.9.cloned.1.call-done), channel_id=1, source_target_pairs={{0,16},{1,17},{2,18},{3,19},{4,20},{5,21},{6,22},{7,23},{8,24},{9,... | collective-permute-start | bytes 2162696 | tf_op jit(solution)/shard_map/ppermute | solution.py:782
  879.3 283.5 %reduce-scatter.23.cloned.1.call-start = ((), (), s32[]{:S(2)}) async-start(), calls=%async_computation.20 | async-start | bytes 3604480 | tf_op jit(solution)/shard_map/reduce_scatter | solution.py:430
  880.5 170.9 %collective-permute-start.132 = (bf16[1,256,512]{2,1,0:T(8,128)(2,1)S(1)}, bf16[1,256,512]{2,1,0:T(8,128)(2,1)}, u32[]{:S(2)}, u32[]{:S(2)}) collective-permute-start(bf16[1,256,512]{2,1,0:T(8,128)(2,1)S(1)} %slice.1429), channel_id=1, source_target_pairs={{0,16},{1,17},{2,18},{3,19},{4,20},{5,21},{6,22},{7,23},{8,24},{9,... | collective-permute-start | bytes 786440 | tf_op jit(solution)/shard_map/ppermute | solution.py:782
  929.3 71.1 %collective-permute-start.102 = (bf16[2,512,512]{2,1,0:T(8,128)(2,1)}, bf16[2,512,512]{2,1,0:T(8,128)(2,1)}, u32[]{:S(2)}, u32[]{:S(2)}) collective-permute-start(bf16[2,512,512]{2,1,0:T(8,128)(2,1)} %add_convert_fusion.2), channel_id=1, source_target_pairs={{4,0},{8,12},{5,1},{9,13},{6,2},{10,14},{7,3},{11,15},{20,16},{24,... | collective-permute-start | bytes 3145736 | tf_op jit(solution)/shard_map/ppermute | solution.py:268
  1023.9 157.8 %reduce-scatter.21.cloned.1.call-start = ((), (), s32[]{:S(2)}) async-start(), calls=%async_computation.19 | async-start | bytes 3932160 | tf_op jit(solution)/shard_map/reduce_scatter | solution.py:430
  1049.7 38.8 %collective-permute-start.119 = (bf16[256,2048]{1,0:T(8,128)(2,1)}, bf16[256,2048]{1,0:T(8,128)(2,1)}, u32[]{:S(2)}, u32[]{:S(2)}) collective-permute-start(bf16[256,2048]{1,0:T(8,128)(2,1)} %reshape.1039), channel_id=1, source_target_pairs={{12,16},{28,20},{8,24},{24,28},{13,17},{29,21},{9,25},{25,29},{14,... | collective-permute-start | bytes 3145736 | tf_op jit(solution)/shard_map/ppermute | solution.py:523
  1075.7 38.5 %collective-permute-start.109 = (bf16[128,2048]{1,0:T(8,128)(2,1)}, bf16[128,2048]{1,0:T(8,128)(2,1)S(1)}, u32[]{:S(2)}, u32[]{:S(2)}) collective-permute-start(bf16[128,2048]{1,0:T(8,128)(2,1)} %reshape.1037), channel_id=1, source_target_pairs={{12,0},{28,4},{8,8},{24,12},{13,1},{29,5},{9,9},{25,13},{14,2},{30... | collective-permute-start | bytes 1572872 | tf_op jit(solution)/shard_map/ppermute | solution.py:523
  1081.8 81.0 %collective-permute-start.134 = (bf16[2,256,1408]{2,1,0:T(8,128)(2,1)}, bf16[2,256,1408]{2,1,0:T(8,128)(2,1)}, u32[]{:S(2)}, u32[]{:S(2)}) collective-permute-start(bf16[2,256,1408]{2,1,0:T(8,128)(2,1)} %pad_maximum_fusion.12), channel_id=1, source_target_pairs={{0,16},{1,17},{2,18},{3,19},{4,20},{5,21},{6,22},{7,23},{8,24},{9,... | collective-permute-start | bytes 4325384 | tf_op jit(solution)/shard_map/ppermute | solution.py:782
  1087.2 41.1 %collective-permute-start.133 = (bf16[1,256,512]{2,1,0:T(8,128)(2,1)}, bf16[1,256,512]{2,1,0:T(8,128)(2,1)}, u32[]{:S(2)}, u32[]{:S(2)}) collective-permute-start(bf16[1,256,512]{2,1,0:T(8,128)(2,1)} %get-tuple-element.459), channel_id=1, source_target_pairs={{16,0},{17,1},{18,2},{19,3},{20,4},{21,5},{22,6},{23,7},{24,8},{25... | collective-permute-start | bytes 786440 | tf_op jit(solution)/shard_map/ppermute | solution.py:781
  1149.1 57.3 %collective-permute-start.130 = (bf16[3,256,512]{2,1,0:T(8,128)(2,1)}, bf16[3,256,512]{2,1,0:T(8,128)(2,1)}, u32[]{:S(2)}, u32[]{:S(2)}) collective-permute-start(bf16[3,256,512]{2,1,0:T(8,128)(2,1)} %reduce-scatter.15.cloned.1.call-done), channel_id=1, source_target_pairs={{0,16},{1,17},{2,18},{3,19},{4,20},{5,21},{6,22},{7,23},{8,24},{9,... | collective-permute-start | bytes 2359304 | tf_op jit(solution)/shard_map/ppermute | solution.py:782
  (339 other events, 4416.3 us)
Sparse Core Ops, SparseCore 0:
  39.7 87.4 all-gather.5
  133.4 156.3 all-gather.9
  291.9 78.9 all-gather.7
  372.9 105.2 all-gather.13
  493.5 65.8 all-gather.11
  561.6 54.8 reduce-scatter.8
  619.6 55.4 reduce-scatter.10
  706.8 75.0 reduce-scatter.12
  784.8 60.6 reduce-scatter.14
  847.6 56.1 reduce-scatter.16
  906.7 88.6 reduce-scatter.18
  1024.1 79.2 reduce-scatter.22
  1106.2 63.8 reduce-scatter.20
